TPU v7x, 512 devices: a whole 4x4x16 slice. The times are simulated.
512 devices in a mesh: fsdp: 16 (over z), ctx: 32 (over x, y, core).
Axes of the slice: x: 4, y: 4, z: 16, core: 2. Of those that a mesh axis runs over, the one named last changes fastest.
Arguments:
- queries: bfloat16 [65536, 2048], P(('fsdp', 'ctx')), may hold values from -320 to 320
- keys: bfloat16 [65536, 2048], P(('fsdp', 'ctx')), may hold values from -5 to 5
- values: bfloat16 [65536, 2048], P(('fsdp', 'ctx')), may hold values from -24 to 24
- out_weight: bfloat16 [2048, 2048], P('fsdp'), may hold values from -0.125 to 0.125
- cotangent: bfloat16 [65536, 2048], P(('fsdp', 'ctx')), may hold values from -6 to 6
- positions: int32 [8192], replicated, may hold values from 0 to 65535, as said below
- global_blocks: int32 [2], replicated, may hold values from 0 to 1023
- random_blocks: int32 [1024, 32, 3], P('fsdp', 'ctx'), may hold values from 0 to 1023, as said below
Outputs:
- context: bfloat16 [65536, 2048], P(('fsdp', 'ctx'))
- grad_queries: bfloat16 [65536, 2048], P(('fsdp', 'ctx'))
- grad_keys: bfloat16 [65536, 2048], P(('fsdp', 'ctx'))
- grad_values: bfloat16 [65536, 2048], P(('fsdp', 'ctx'))
Inputs may be any that keep to these rules, and one draw needn't show every extreme that they name: random_blocks[i, h, r] lies in the same aligned run of 64 blocks as i. `positions`: the first and the last block of every aligned run of 64 blocks hold at least one listed position.
All inputs are finite; a program needn't handle non-finite values.
Results may differ from a plain program's by a relative error of at most 0.008.
Values may be sent and summed in bfloat16 or wider, within the bound.
A program may use at most 64 MiB of HBM per device.

v0:
```python
import math

import jax
import jax.numpy as jnp
from jax import lax
from jax.sharding import PartitionSpec as P

HD = 64
BLK = 64
GLOB = 2


def padded_2(block, sides, width):
    for axis, dim in sides:
        count = lax.axis_size(axis)
        forward = [(i, i + 1) for i in range(count - 1)]
        backward = [(target, source) for source, target in forward]
        low = lax.ppermute(
            lax.slice_in_dim(block, block.shape[dim] - width, None, axis=dim), axis, forward
        )
        high = lax.ppermute(lax.slice_in_dim(block, 0, width, axis=dim), axis, backward)
        block = jnp.concatenate([low, block, high], axis=dim)
    return block


def add_rows(total, rows, begin):
    current = lax.dynamic_slice_in_dim(total, begin, rows.shape[0], 0)
    return lax.dynamic_update_slice_in_dim(total, current + rows, begin, 0)


def split_product(selector, terms):
    contract_first = (((0,), (0,)), ((), ()))
    high = terms.astype(jnp.bfloat16)
    low = (terms - high.astype(jnp.float32)).astype(jnp.bfloat16)
    first = lax.dot_general(selector, high, contract_first, preferred_element_type=jnp.float32)
    return first + lax.dot_general(
        selector, low, contract_first, preferred_element_type=jnp.float32
    )


def head_pass(query_blocks, key_ext, value_ext, grad_blocks, ext_ids, usable):
    block_count = query_blocks.shape[0]
    ext_count = key_ext.shape[0]
    slot_count = ext_ids.shape[1]
    per_step = min(block_count, max(1, 512 // BLK))
    turns = block_count // per_step
    factor = 1.0 / math.sqrt(HD)
    catalog = jnp.arange(block_count, dtype=jnp.int32)
    far_start = 3 + GLOB

    def advance(totals, packed):
        key_sum, value_sum = totals
        turn, query_part, grad_part, ids_part, usable_part = packed
        key_group = key_ext[ids_part].reshape(per_step, slot_count * BLK, HD)
        value_group = value_ext[ids_part].reshape(per_step, slot_count * BLK, HD)
        keymask = jnp.repeat(usable_part, BLK, axis=1)[:, None, :]
        scores = (
            jnp.einsum("nqd,nkd->nqk", query_part, key_group, preferred_element_type=jnp.float32)
            * factor
        )
        scores = jnp.where(keymask, scores, -1e30)
        highest = jnp.max(scores, axis=-1, keepdims=True)
        raised = jnp.where(keymask, jnp.exp(scores - highest), 0.0)
        probs = raised / jnp.sum(raised, axis=-1, keepdims=True)
        probs_half = probs.astype(jnp.bfloat16)
        context = jnp.einsum(
            "nqk,nkd->nqd", probs_half, value_group, preferred_element_type=jnp.float32
        ).astype(jnp.bfloat16)
        grad_probs = jnp.einsum(
            "nqd,nkd->nqk", grad_part, value_group, preferred_element_type=jnp.float32
        )
        inner = jnp.sum(probs * grad_probs, axis=-1, keepdims=True)
        grad_scores = (probs * (grad_probs - inner) * factor).astype(jnp.bfloat16)
        grad_query = jnp.einsum(
            "nqk,nkd->nqd", grad_scores, key_group, preferred_element_type=jnp.float32
        ).astype(jnp.bfloat16)
        key_terms = jnp.einsum(
            "nqk,nqd->nkd", grad_scores, query_part, preferred_element_type=jnp.float32
        )
        value_terms = jnp.einsum(
            "nqk,nqd->nkd", probs_half, grad_part, preferred_element_type=jnp.float32
        )
        weight = usable_part.astype(jnp.float32)[:, :, None]
        key_terms = key_terms.reshape(per_step, slot_count, BLK * HD) * weight
        value_terms = value_terms.reshape(per_step, slot_count, BLK * HD) * weight
        begin = turn * per_step
        for slot in range(3):
            key_sum = add_rows(key_sum, key_terms[:, slot], begin + slot)
            value_sum = add_rows(value_sum, value_terms[:, slot], begin + slot)
        key_sum = key_sum.at[block_count + 2 : block_count + 2 + GLOB].add(
            jnp.sum(key_terms[:, 3:far_start], axis=0)
        )
        value_sum = value_sum.at[block_count + 2 : block_count + 2 + GLOB].add(
            jnp.sum(value_terms[:, 3:far_start], axis=0)
        )
        far_ids = ids_part[:, far_start:].reshape(-1) - 1
        selector = (far_ids[:, None] == catalog[None, :]).astype(jnp.bfloat16)
        far_keys = key_terms[:, far_start:].reshape(-1, BLK * HD)
        far_values = value_terms[:, far_start:].reshape(-1, BLK * HD)
        key_sum = key_sum.at[1 : block_count + 1].add(split_product(selector, far_keys))
        value_sum = value_sum.at[1 : block_count + 1].add(split_product(selector, far_values))
        return ((key_sum, value_sum), (context, grad_query))

    packed_all = (
        jnp.arange(turns, dtype=jnp.int32),
        query_blocks.reshape(turns, per_step, BLK, HD),
        grad_blocks.reshape(turns, per_step, BLK, HD),
        ext_ids.reshape(turns, per_step, slot_count),
        usable.reshape(turns, per_step, slot_count),
    )
    start_sums = (
        jnp.zeros((ext_count, BLK * HD), jnp.float32),
        jnp.zeros((ext_count, BLK * HD), jnp.float32),
    )
    final_sums, outputs = lax.scan(advance, start_sums, packed_all)
    context = outputs[0].reshape(block_count, BLK, HD)
    grad_query = outputs[1].reshape(block_count, BLK, HD)
    key_sums = final_sums[0].reshape(ext_count, BLK, HD)
    value_sums = final_sums[1].reshape(ext_count, BLK, HD)
    return (context, grad_query, key_sums, value_sums)


def run_head(packed):
    return head_pass(packed[0], packed[1], packed[2], packed[3], packed[4], packed[5])


def body(queries, keys, values, out_weight, cotangent, positions, global_blocks, random_blocks):
    rows_here = queries.shape[0]
    offset = (lax.axis_index("fsdp") * lax.axis_size("ctx") + lax.axis_index("ctx")) * rows_here
    places = offset + jnp.arange(rows_here, dtype=jnp.int32)
    masked = jnp.any(positions[:, None] == places[None, :], axis=0)
    upstream = jnp.where(masked[:, None], cotangent, jnp.zeros_like(cotangent))
    contract_last = (((1,), (1,)), ((), ()))
    grad_context = lax.dot_general(
        upstream,
        lax.all_gather(out_weight, "fsdp", axis=0, tiled=True),
        contract_last,
        preferred_element_type=jnp.float32,
    ).astype(jnp.bfloat16)
    head_query, head_key, head_value = (
        lax.all_to_all(queries, "ctx", split_axis=1, concat_axis=0, tiled=True),
        lax.all_to_all(keys, "ctx", split_axis=1, concat_axis=0, tiled=True),
        lax.all_to_all(values, "ctx", split_axis=1, concat_axis=0, tiled=True),
    )
    head_grad = lax.all_to_all(grad_context, "ctx", split_axis=1, concat_axis=0, tiled=True)
    seg_len = head_query.shape[0]
    local_blocks = seg_len // BLK
    head_count = head_query.shape[1] // HD
    group = lax.axis_index("fsdp")
    block_total = local_blocks * lax.axis_size("fsdp")
    first_block = group * local_blocks
    pair = jnp.stack([head_key, head_value])
    padded = padded_2(pair, (("fsdp", 1),), BLK)
    owner = global_blocks // local_blocks
    spot = global_blocks % local_blocks
    picks = []
    for which in range(GLOB):
        piece = lax.dynamic_slice_in_dim(pair, spot[which] * BLK, BLK, 1)
        picks.append(
            jnp.where(owner[which] == group, piece, jnp.zeros_like(piece)).astype(jnp.float32)
        )
    shared = lax.psum(jnp.concatenate(picks, axis=1).astype(jnp.bfloat16), "fsdp")
    extended = jnp.concatenate([padded, shared], axis=1)
    ext_rows = extended.shape[1]
    local_ids = jnp.arange(local_blocks, dtype=jnp.int32)
    current = first_block + local_ids
    window = jnp.stack([current - 1, current, current + 1], axis=1)
    window = window[:, None, :]
    globals_wide = jnp.broadcast_to(global_blocks[None, None, :], (local_blocks, head_count, GLOB))
    slot_ids = jnp.concatenate([window, globals_wide, random_blocks], axis=2)
    slot_count = slot_ids.shape[2]
    inside = (slot_ids >= 0) & (slot_ids < block_total)
    order = jnp.arange(slot_count)
    earlier = order[None, :] < order[:, None]
    repeated = jnp.any((slot_ids[..., :, None] == slot_ids[..., None, :]) & earlier, axis=-1)
    usable = inside & jnp.logical_not(repeated)
    near = jnp.stack([local_ids, local_ids + 1, local_ids + 2], axis=1)
    near = near[:, None, :]
    far = local_blocks + 2 + jnp.arange(GLOB, dtype=jnp.int32)
    far = jnp.broadcast_to(far[None, None, :], (local_blocks, head_count, GLOB))
    picked = random_blocks - first_block + 1
    ext_ids = jnp.concatenate([near, far, picked], axis=2)

    def to_heads(rows):
        return rows.reshape(rows.shape[0] // BLK, BLK, head_count, HD).transpose(2, 0, 1, 3)

    def from_heads(blocks):
        return blocks.transpose(1, 2, 0, 3).reshape(blocks.shape[1] * BLK, head_count * HD)

    results = lax.map(
        run_head,
        (
            to_heads(head_query),
            to_heads(extended[0]),
            to_heads(extended[1]),
            to_heads(head_grad),
            ext_ids.transpose(1, 0, 2),
            usable.transpose(1, 0, 2),
        ),
    )
    sums = jnp.stack([from_heads(results[2]), from_heads(results[3])])
    edges = jnp.concatenate([sums[:, :BLK], sums[:, BLK + seg_len : 2 * BLK + seg_len]], axis=1)
    beside_all = padded_2(edges, (("fsdp", 1),), BLK)
    local = sums[:, BLK : BLK + seg_len]
    local = local.at[:, :BLK].add(beside_all[:, :BLK])
    local = local.at[:, seg_len - BLK :].add(beside_all[:, 3 * BLK :])
    global_sums = lax.psum(sums[:, 2 * BLK + seg_len : ext_rows], "fsdp")
    for which in range(GLOB):
        term = global_sums[:, which * BLK : (which + 1) * BLK]
        term = jnp.where(owner[which] == group, term, jnp.zeros_like(term))
        begin = spot[which] * BLK
        current_rows = lax.dynamic_slice_in_dim(local, begin, BLK, 1)
        local = lax.dynamic_update_slice_in_dim(local, current_rows + term, begin, 1)
    grad_key = local[0].astype(jnp.bfloat16)
    grad_value = local[1].astype(jnp.bfloat16)
    context = lax.all_to_all(from_heads(results[0]), "ctx", split_axis=0, concat_axis=1, tiled=True)
    grad_query, grad_key, grad_value = (
        lax.all_to_all(from_heads(results[1]), "ctx", split_axis=0, concat_axis=1, tiled=True),
        lax.all_to_all(grad_key, "ctx", split_axis=0, concat_axis=1, tiled=True),
        lax.all_to_all(grad_value, "ctx", split_axis=0, concat_axis=1, tiled=True),
    )
    return (context, grad_query, grad_key, grad_value)


def solution(mesh):
    return jax.shard_map(
        body,
        mesh=mesh,
        in_specs=(
            P(("fsdp", "ctx"), None),
            P(("fsdp", "ctx"), None),
            P(("fsdp", "ctx"), None),
            P("fsdp", None),
            P(("fsdp", "ctx"), None),
            P(),
            P(),
            P("fsdp", "ctx", None),
        ),
        out_specs=(
            P(("fsdp", "ctx"), None),
            P(("fsdp", "ctx"), None),
            P(("fsdp", "ctx"), None),
            P(("fsdp", "ctx"), None),
        ),
        check_vma=False,
    )
```

profile of v0, /device:TPU:1, one launch (start us, length us, event | category | flops | bytes accessed | tf_op | source)
XLA Modules:
  0.0 887.6 jit_solution(4406195249932147159)
XLA Ops:
  10.0 10.6 %all-to-all-start.1 = ((bf16[128,32,64]{0,2,1:T(8,128)(2,1)}), bf16[128,32,64]{0,2,1:T(8,128)(2,1)S(1)}, u32[]{:S(2)}, u32[]{:S(2)}) async-start(bf16[128,32,64]{0,2,1:T(8,128)(2,1)} %bitcast.7), calls=%async_computation.1 | async-start | bytes 1048576 | tf_op jit(solution)/shard_map/all_to_all | solution.py:142
  22.7 9.7 %all-to-all-done.1 = bf16[128,32,64]{0,2,1:T(8,128)(2,1)S(1)} async-done(((bf16[128,32,64]{0,2,1:T(8,128)(2,1)}), bf16[128,32,64]{0,2,1:T(8,128)(2,1)S(1)}, u32[]{:S(2)}, u32[]{:S(2)}) %all-to-all-start.1) | async-done | bytes 524320 | tf_op jit(solution)/shard_map/all_to_all | solution.py:142
  47.5 5.0 all-to-all-start
  54.6 4.0 collective-permute-start
  58.7 53.3 %psum.14 = bf16[2,128,64]{1,2,0:T(8,128)(2,1)S(1)} all-reduce(bf16[2,128,64]{1,2,0:T(8,128)(2,1)S(1)} %pad_maximum_fusion.1), channel_id=1, replica_groups=mesh['fsdp'=16,'ctx'=32] {'fsdp'}, use_global_device_ids=true, to_apply=%region_2.3 | all-reduce | flops 16384 | bytes 65536 | tf_op jit(solution)/shard_map/psum | solution.py:162
  115.0 7.7 all-gather.2.cloned.1.call-done
  122.8 6.3 convolution_convert_fusion.2
  130.1 8.0 all-to-all-start.3
  141.0 8.8 all-to-all-done.3
  153.3 526.1 %while.39 = (s32[]{:T(128)}, f32[68,4096]{1,0:T(8,128)}, f32[68,4096]{1,0:T(8,128)}, bf16[8,8,64,64]{3,2,1,0:T(8,128)(2,1)}, bf16[8,8,64,64]{3,2,1,0:T(8,128)(2,...) while((s32[]{:T(128)}, f32[68,4096]{1,0:T(8,128)}, ...), condition=%wide.region_9.10_spmd.clone, body=%wide.region_3.9_spmd.clone.sunk | while | flops 261697312 | bytes 74529592 | solution.py:115
  164.2 5.8 fusion.163
  169.9 7.3 fusion.150
  211.6 3.9 scatter-add.44
  230.0 5.7 fusion.163
  235.7 7.3 fusion.150
  295.7 5.7 fusion.163
  301.5 7.3 fusion.150
  361.5 5.7 fusion.163
  367.2 7.3 fusion.150
  427.3 5.7 fusion.163
  433.0 7.3 fusion.150
  493.1 5.7 fusion.163
  498.8 7.3 fusion.150
  558.8 5.7 fusion.163
  564.6 7.3 fusion.150
  624.6 5.7 fusion.163
  630.3 7.3 fusion.150
  708.7 4.7 all-to-all-start.4
  713.4 112.9 %all-reduce.2.cloned.1.call-done = f32[2,128,64]{1,2,0:T(8,128)} async-done(((f32[2,128,64]{1,2,0:T(8,128)}), f32[2,128,64]{1,2,0:T(8,128)}) %all-reduce.2.cloned.1.call-update) | async-done | bytes 65552 | tf_op jit(solution)/shard_map/psum | solution.py:207
  834.3 18.6 %all-to-all-start.7 = ((bf16[32,128,64]{1,2,0:T(8,128)(2,1)}), bf16[32,128,64]{1,2,0:T(8,128)(2,1)S(1)}, u32[]{:S(2)}, u32[]{:S(2)}) async-start(bf16[32,128,64]{1,2,0:T(8,128)(2,1)} %copy.262), calls=%async_computation.7 | async-start | bytes 1048576 | tf_op jit(solution)/shard_map/all_to_all | solution.py:220
  854.0 10.5 %all-to-all-done.7 = bf16[32,128,64]{1,2,0:T(8,128)(2,1)S(1)} async-done(((bf16[32,128,64]{1,2,0:T(8,128)(2,1)}), bf16[32,128,64]{1,2,0:T(8,128)(2,1)S(1)}, u32[]{:S(2)}, u32[]{:S(2)}) %all-to-all-start.7) | async-done | bytes 524320 | tf_op jit(solution)/shard_map/all_to_all | solution.py:220
  871.2 8.5 all-to-all-done.6
  (621 shorter events, 487.1 us)
Async XLA Ops:
  7.2 115.6 %all-gather.2.cloned.1.call-start = ((), (), s32[]{:S(2)}) async-start(), calls=%async_computation.8 | async-start | bytes 8912896 | tf_op jit(solution)/shard_map/all_gather | solution.py:136
  7.9 12.7 %copy-start.9 = (bf16[128,2048]{1,0:T(8,128)(2,1)S(1)}, bf16[128,2048]{1,0:T(8,128)(2,1)}, u32[]{:S(2)}) copy-start(bf16[128,2048]{1,0:T(8,128)(2,1)} %param.24) | copy-start | bytes 1572868
  10.0 11.6 %copy-start.15 = (s32[2]{0:T(128)S(1)}, s32[2]{0:T(128)}, u32[]{:S(2)}) copy-start(s32[2]{0:T(128)} %param.28) | copy-start | bytes 28
  10.0 12.5 %copy-start.14 = (s32[64,1,3]{0,1,2:T(1,128)S(1)}, s32[64,1,3]{0,1,2:T(1,128)}, u32[]{:S(2)}) copy-start(s32[64,1,3]{0,1,2:T(1,128)} %param.29) | copy-start | bytes 2308
  10.0 22.3 %all-to-all-start.1 = ((bf16[128,32,64]{0,2,1:T(8,128)(2,1)}), bf16[128,32,64]{0,2,1:T(8,128)(2,1)S(1)}, u32[]{:S(2)}, u32[]{:S(2)}) async-start(bf16[128,32,64]{0,2,1:T(8,128)(2,1)} %bitcast.7), calls=%async_computation.1 | async-start | bytes 1048576 | tf_op jit(solution)/shard_map/all_to_all | solution.py:142
  20.6 19.0 %copy-start.10 = (bf16[128,2048]{1,0:T(8,128)(2,1)S(1)}, bf16[128,2048]{1,0:T(8,128)(2,1)}, u32[]{:S(2)}) copy-start(bf16[128,2048]{1,0:T(8,128)(2,1)} %param.22) | copy-start | bytes 1572868
  32.3 15.2 %all-to-all-start.2 = ((bf16[128,32,64]{0,2,1:T(8,128)(2,1)}), bf16[128,32,64]{0,2,1:T(8,128)(2,1)S(1)}, u32[]{:S(2)}, u32[]{:S(2)}) async-start(bf16[128,32,64]{0,2,1:T(8,128)(2,1)} %bitcast.9), calls=%async_computation.2 | async-start | bytes 1048576 | tf_op jit(solution)/shard_map/all_to_all | solution.py:143
  47.5 64.4 %all-to-all-start = ((bf16[128,32,64]{0,2,1:T(8,128)(2,1)}), bf16[128,32,64]{0,2,1:T(8,128)(2,1)S(1)}, u32[]{:S(2)}, u32[]{:S(2)}) async-start(bf16[128,32,64]{0,2,1:T(8,128)(2,1)} %bitcast.3), calls=%async_computation | async-start | bytes 1048576 | tf_op jit(solution)/shard_map/all_to_all | solution.py:141
  53.3 60.1 %collective-permute-start.1 = (bf16[2,64,64]{1,2,0:T(8,128)(2,1)S(1)}, bf16[2,64,64]{1,2,0:T(8,128)(2,1)S(1)}, u32[]{:S(2)}, u32[]{:S(2)}) collective-permute-start(bf16[2,64,64]{1,2,0:T(8,128)(2,1)S(1)} %get-tuple-element.476), channel_id=1, source_target_pairs={{32,0},{64,32},{96,64},{128,96},{160,128},{192,160},{224,192},{256... | collective-permute-start | bytes 49160 | tf_op jit(solution)/shard_map/ppermute | solution.py:21
  54.6 58.8 %collective-permute-start = (bf16[2,64,64]{1,2,0:T(8,128)(2,1)S(1)}, bf16[2,64,64]{1,2,0:T(8,128)(2,1)S(1)}, u32[]{:S(2)}, u32[]{:S(2)}) collective-permute-start(bf16[2,64,64]{1,2,0:T(8,128)(2,1)S(1)} %get-tuple-element.477), channel_id=1, source_target_pairs={{0,32},{32,64},{64,96},{96,128},{128,160},{160,192},{192,224},{224... | collective-permute-start | bytes 49160 | tf_op jit(solution)/shard_map/ppermute | solution.py:18
  113.4 9.4 %copy-start.8 = (bf16[128,2048]{1,0:T(8,128)(2,1)S(1)}, bf16[128,2048]{1,0:T(8,128)(2,1)}, u32[]{:S(2)}) copy-start(bf16[128,2048]{1,0:T(8,128)(2,1)} %param.26) | copy-start | bytes 1572868
  130.1 19.7 %all-to-all-start.3 = ((bf16[128,32,64]{0,2,1:T(8,128)(2,1)}), bf16[128,32,64]{0,2,1:T(8,128)(2,1)S(1)}, u32[]{:S(2)}, u32[]{:S(2)}) async-start(bf16[128,32,64]{0,2,1:T(8,128)(2,1)} %bitcast.16), calls=%async_computation.3 | async-start | bytes 1048576 | tf_op jit(solution)/shard_map/all_to_all | solution.py:145
  192.4 7.1 copy-start.6
  196.9 11.1 %copy-start.5 = (f32[2,4096]{1,0:T(2,128)S(1)}, f32[2,4096]{1,0:T(2,128)}, u32[]{:S(2)}) copy-start(f32[2,4096]{1,0:T(2,128)} %get-tuple-element.582) | copy-start | bytes 98308 | tf_op jit(solution)/shard_map/while/body/eval_jaxpr/while
  262.6 11.2 %copy-start.5 = (f32[2,4096]{1,0:T(2,128)S(1)}, f32[2,4096]{1,0:T(2,128)}, u32[]{:S(2)}) copy-start(f32[2,4096]{1,0:T(2,128)} %get-tuple-element.582) | copy-start | bytes 98308 | tf_op jit(solution)/shard_map/while/body/eval_jaxpr/while
  324.0 7.1 copy-start.6
  328.4 11.1 %copy-start.5 = (f32[2,4096]{1,0:T(2,128)S(1)}, f32[2,4096]{1,0:T(2,128)}, u32[]{:S(2)}) copy-start(f32[2,4096]{1,0:T(2,128)} %get-tuple-element.582) | copy-start | bytes 98308 | tf_op jit(solution)/shard_map/while/body/eval_jaxpr/while
  389.8 7.1 copy-start.6
  394.2 11.1 %copy-start.5 = (f32[2,4096]{1,0:T(2,128)S(1)}, f32[2,4096]{1,0:T(2,128)}, u32[]{:S(2)}) copy-start(f32[2,4096]{1,0:T(2,128)} %get-tuple-element.582) | copy-start | bytes 98308 | tf_op jit(solution)/shard_map/while/body/eval_jaxpr/while
  455.5 7.1 copy-start.6
  460.0 11.1 %copy-start.5 = (f32[2,4096]{1,0:T(2,128)S(1)}, f32[2,4096]{1,0:T(2,128)}, u32[]{:S(2)}) copy-start(f32[2,4096]{1,0:T(2,128)} %get-tuple-element.582) | copy-start | bytes 98308 | tf_op jit(solution)/shard_map/while/body/eval_jaxpr/while
  521.3 7.1 copy-start.6
  525.8 11.1 %copy-start.5 = (f32[2,4096]{1,0:T(2,128)S(1)}, f32[2,4096]{1,0:T(2,128)}, u32[]{:S(2)}) copy-start(f32[2,4096]{1,0:T(2,128)} %get-tuple-element.582) | copy-start | bytes 98308 | tf_op jit(solution)/shard_map/while/body/eval_jaxpr/while
  591.5 11.1 %copy-start.5 = (f32[2,4096]{1,0:T(2,128)S(1)}, f32[2,4096]{1,0:T(2,128)}, u32[]{:S(2)}) copy-start(f32[2,4096]{1,0:T(2,128)} %get-tuple-element.582) | copy-start | bytes 98308 | tf_op jit(solution)/shard_map/while/body/eval_jaxpr/while
  657.3 11.1 %copy-start.5 = (f32[2,4096]{1,0:T(2,128)S(1)}, f32[2,4096]{1,0:T(2,128)}, u32[]{:S(2)}) copy-start(f32[2,4096]{1,0:T(2,128)} %get-tuple-element.582) | copy-start | bytes 98308 | tf_op jit(solution)/shard_map/while/body/eval_jaxpr/while
  688.9 8.2 collective-permute-start.2
  693.4 15.3 %all-to-all-start.5 = ((bf16[32,128,64]{1,2,0:T(8,128)(2,1)}), bf16[32,128,64]{1,2,0:T(8,128)(2,1)S(1)}, u32[]{:S(2)}, u32[]{:S(2)}) async-start(bf16[32,128,64]{1,2,0:T(8,128)(2,1)} %copy.258), calls=%async_computation.5 | async-start | bytes 1048576 | tf_op jit(solution)/shard_map/all_to_all | solution.py:218
  697.1 129.2 %all-reduce.2.cloned.1.call-start = ((), (), s32[]{:S(2)}) async-start(), calls=%async_computation.9 | async-start | bytes 131072 | tf_op jit(solution)/shard_map/psum | solution.py:207
  697.3 5.9 collective-permute-start.3
  708.7 125.6 %all-to-all-start.4 = ((bf16[32,128,64]{1,2,0:T(8,128)(2,1)}), bf16[32,128,64]{1,2,0:T(8,128)(2,1)S(1)}, u32[]{:S(2)}, u32[]{:S(2)}) async-start(bf16[32,128,64]{1,2,0:T(8,128)(2,1)} %copy.256), calls=%async_computation.4 | async-start | bytes 1048576 | tf_op jit(solution)/shard_map/all_to_all | solution.py:216
  834.3 30.2 %all-to-all-start.7 = ((bf16[32,128,64]{1,2,0:T(8,128)(2,1)}), bf16[32,128,64]{1,2,0:T(8,128)(2,1)S(1)}, u32[]{:S(2)}, u32[]{:S(2)}) async-start(bf16[32,128,64]{1,2,0:T(8,128)(2,1)} %copy.262), calls=%async_computation.7 | async-start | bytes 1048576 | tf_op jit(solution)/shard_map/all_to_all | solution.py:220
  864.5 15.3 %all-to-all-start.6 = ((bf16[32,128,64]{1,2,0:T(8,128)(2,1)}), bf16[32,128,64]{1,2,0:T(8,128)(2,1)S(1)}, u32[]{:S(2)}, u32[]{:S(2)}) async-start(bf16[32,128,64]{1,2,0:T(8,128)(2,1)} %copy.261), calls=%async_computation.6 | async-start | bytes 1048576 | tf_op jit(solution)/shard_map/all_to_all | solution.py:219
  (54 other events, 112.7 us)
Sparse Core Ops, SparseCore 0:
  10.1 112.6 all-gather.1
  701.7 124.5 all-reduce.1
where the time goes:
time: 895 us; the launch traced here: 888 us
  local copies, waits for them, and re-layouts  265 us (30%)
  matrix products  206 us (23%)
  waiting for transfers between devices  164 us (18%)
  other arithmetic  109 us (12%)
  starting transfers between devices  65.9 us (7%)
  blocking collectives  53.3 us (6%)
  between operations  17 us (2%)
    psum x1, waiting for transfers between devices, body(): global_sums = lax.psum(sums[:, 2 * BLK + seg_len:ext_rows], 'fsdp')  113 us
    dynamic_update_slice x48, local copies, waits for them, and re-layouts, add_rows(): return lax.dynamic_update_slice_in_dim(total, current + rows, begin, 0)  80.8 us
    dot_general x8, matrix products, advance(): jnp.einsum('nqk,nqd->nkd', grad_scores, query_part, preferred_element_typ...  58.1 us
    psum x1, blocking collectives, body(): lax.psum(jnp.concatenate(picks, axis=1).astype(jnp.bfloat16), 'fsdp')  53.3 us
    dot_general x8, matrix products, advance(): jnp.einsum('nqk,nkd->nqd', grad_scores, key_group, preferred_element_type...  45.9 us
    add x40, other arithmetic, add_rows(): return lax.dynamic_update_slice_in_dim(total, current + rows, begin, 0)  44.9 us
    scatter-add x8, local copies, waits for them, and re-layouts, advance(): key_sum.at[1:block_count + 1].add(split_product(selector, far_keys))  31.6 us
    dot_general x8, matrix products, advance(): jnp.einsum('nqk,nqd->nkd', probs_half, grad_part, preferred_element_type=...  29 us
  transfers between devices with their start and end apart: 14, of which 8 were waited for; matrix products, arithmetic and copies ran while one was open for 4% of the time, Pallas kernels for 0%

commit v1 on v0

v1 whole, which is shorter than its diff:
```python
import functools
import math

import jax
import jax.numpy as jnp
from jax import lax
from jax.experimental import pallas as pl
from jax.experimental.pallas import tpu as pltpu
from jax.sharding import PartitionSpec as P

HD = 64
BLK = 64
GLOB = 2
SLOTS = 8


def contract(a, b, da, db):
    return lax.dot_general(a, b, (((da,), (db,)), ((), ())), preferred_element_type=jnp.float32)


def attend_kernel(pairs, ids_ref, kv_ref, qg_ref, bias_ref, dqo_ref, dkv_ref):
    width = 2 * HD
    scale = math.log2(math.e) / math.sqrt(HD)
    low = lax.broadcasted_iota(jnp.int32, (BLK, width), 1) < HD
    zero = jnp.zeros((BLK, width), jnp.bfloat16)
    dkv_ref[...] = jnp.zeros_like(dkv_ref)
    blocks = kv_ref.shape[0] // BLK

    def rows(block):
        return pl.ds(pl.multiple_of(block * BLK, BLK), BLK)

    def step(j, carry):
        first = qg_ref[rows(2 * j), :]
        second = qg_ref[rows(2 * j + 1), :]
        mixed = jnp.concatenate(
            [
                jnp.concatenate([jnp.where(low, first, zero), zero], axis=1),
                jnp.concatenate([zero, jnp.where(low, second, zero)], axis=1),
                jnp.concatenate([jnp.where(low, zero, first), zero], axis=1),
                jnp.concatenate([zero, jnp.where(low, zero, second)], axis=1),
            ],
            axis=0,
        )
        left = [ids_ref[2 * j, s] for s in range(SLOTS)]
        right = [ids_ref[2 * j + 1, s] for s in range(SLOTS)]
        both = jnp.concatenate(
            [
                jnp.concatenate([kv_ref[rows(a), :], kv_ref[rows(b), :]], axis=1)
                for a, b in zip(left, right)
            ],
            axis=0,
        )
        products = contract(both, mixed, 1, 1)
        scores = []
        for s in range(SLOTS):
            part = products[s * BLK : (s + 1) * BLK, :width]
            scores.append(part * scale + bias_ref[pl.ds(j * SLOTS + s, 1), :])
        highest = functools.reduce(jnp.maximum, scores)
        highest = jnp.max(highest, axis=0, keepdims=True)
        raised = [jnp.exp2(part - highest) for part in scores]
        total = jnp.sum(functools.reduce(jnp.add, raised), axis=0, keepdims=True)
        inverse = 1.0 / total
        probs = [part * inverse for part in raised]
        grads = [products[s * BLK : (s + 1) * BLK, width:] for s in range(SLOTS)]
        inner = functools.reduce(jnp.add, [p * g for p, g in zip(probs, grads)])
        inner = jnp.sum(inner, axis=0, keepdims=True)
        weights = jnp.concatenate(
            [
                jnp.concatenate(
                    [(p * (g - inner)).astype(jnp.bfloat16), p.astype(jnp.bfloat16)], axis=1
                )
                for p, g in zip(probs, grads)
            ],
            axis=0,
        )
        sums = contract(weights, both, 0, 0)
        eighth = jnp.where(low, 1.0 / math.sqrt(HD), 1.0)
        out_first = jnp.where(low, sums[:BLK, :width], sums[2 * BLK : 3 * BLK, :width]) * eighth
        out_second = jnp.where(low, sums[BLK : 2 * BLK, width:], sums[3 * BLK :, width:]) * eighth
        dqo_ref[rows(2 * j), :] = out_first.astype(jnp.bfloat16)
        dqo_ref[rows(2 * j + 1), :] = out_second.astype(jnp.bfloat16)
        terms = contract(weights, mixed, 1, 0)

        def term(s, side):
            return terms[s * BLK : (s + 1) * BLK, side * width : (side + 1) * width]

        dkv_ref[rows(2 * j), :] += term(0, 0)
        dkv_ref[rows(2 * j + 1), :] += term(1, 0) + term(0, 1)
        dkv_ref[rows(2 * j + 2), :] += term(2, 0) + term(1, 1)
        dkv_ref[rows(2 * j + 3), :] += term(2, 1)
        for s in range(3, 3 + GLOB):
            dkv_ref[rows(blocks - GLOB + s - 3), :] += term(s, 0) + term(s, 1)
        for s in range(3 + GLOB, SLOTS):
            dkv_ref[rows(left[s]), :] += term(s, 0)
            dkv_ref[rows(right[s]), :] += term(s, 1)
        return carry

    lax.fori_loop(0, pairs, step, 0)
    eighth = jnp.where(low, 1.0 / math.sqrt(HD), 1.0)

    def finish(b, carry):
        dkv_ref[rows(b), :] = dkv_ref[rows(b), :] * eighth
        return carry

    lax.fori_loop(0, blocks, finish, 0)


def attend(ids, kv, qg, bias):
    pairs = qg.shape[0] // (2 * BLK)
    vmem = pl.BlockSpec(memory_space=pltpu.VMEM)
    return pl.pallas_call(
        functools.partial(attend_kernel, pairs),
        out_shape=(
            jax.ShapeDtypeStruct(qg.shape, jnp.bfloat16),
            jax.ShapeDtypeStruct(kv.shape, jnp.float32),
        ),
        in_specs=[pl.BlockSpec(memory_space=pltpu.SMEM), vmem, vmem, vmem],
        out_specs=(vmem, vmem),
        compiler_params=pltpu.CompilerParams(vmem_limit_bytes=48 * 1024 * 1024),
    )(ids, kv, qg, bias)


def neighbours(block, dim, width):
    count = lax.axis_size("fsdp")
    forward = [(i, i + 1) for i in range(count - 1)]
    backward = [(target, source) for source, target in forward]
    last = lax.slice_in_dim(block, block.shape[dim] - width, None, axis=dim)
    low = lax.ppermute(last, "fsdp", forward)
    high = lax.ppermute(lax.slice_in_dim(block, 0, width, axis=dim), "fsdp", backward)
    return low, high


def pack(a, b):
    heads = a.shape[1] // HD
    both = jnp.stack([a.reshape(-1, heads, HD), b.reshape(-1, heads, HD)], axis=2)
    return both.reshape(a.shape[0], 2 * a.shape[1])


def unpack(both):
    heads = both.shape[1] // (2 * HD)
    split = both.reshape(-1, heads, 2, HD)
    return split[:, :, 0].reshape(-1, heads * HD), split[:, :, 1].reshape(-1, heads * HD)


def tables(global_blocks, random_blocks, local_blocks):
    group = lax.axis_index("fsdp")
    first_block = group * local_blocks
    block_total = local_blocks * lax.axis_size("fsdp")
    local_ids = jnp.arange(local_blocks, dtype=jnp.int32)
    current = first_block + local_ids
    window = jnp.stack([current - 1, current, current + 1], axis=1)
    globals_wide = jnp.broadcast_to(global_blocks[None, :], (local_blocks, GLOB))
    slot_ids = jnp.concatenate([window, globals_wide, random_blocks], axis=1)
    inside = (slot_ids >= 0) & (slot_ids < block_total)
    order = jnp.arange(SLOTS)
    earlier = order[None, :] < order[:, None]
    repeated = jnp.any((slot_ids[:, :, None] == slot_ids[:, None, :]) & earlier, axis=-1)
    usable = inside & jnp.logical_not(repeated)
    near = jnp.stack([local_ids, local_ids + 1, local_ids + 2], axis=1)
    far = local_blocks + 2 + jnp.arange(GLOB, dtype=jnp.int32)
    far = jnp.broadcast_to(far[None, :], (local_blocks, GLOB))
    ids = jnp.concatenate([near, far, random_blocks - first_block + 1], axis=1)
    bias = jnp.where(usable, 0.0, -1e30).astype(jnp.float32)
    bias = bias.reshape(local_blocks // 2, 2, SLOTS).transpose(0, 2, 1)
    bias = jnp.repeat(bias.reshape(-1, 2), BLK, axis=1)
    return ids, bias


def body(queries, keys, values, out_weight, cotangent, positions, global_blocks, random_blocks):
    rows_here = queries.shape[0]
    offset = (lax.axis_index("fsdp") * lax.axis_size("ctx") + lax.axis_index("ctx")) * rows_here
    places = offset + jnp.arange(rows_here, dtype=jnp.int32)
    masked = jnp.any(positions[:, None] == places[None, :], axis=0)
    upstream = jnp.where(masked[:, None], cotangent, jnp.zeros_like(cotangent))
    grad_context = contract(
        upstream, lax.all_gather(out_weight, "fsdp", axis=0, tiled=True), 1, 1
    ).astype(jnp.bfloat16)
    kv = lax.all_to_all(pack(keys, values), "ctx", split_axis=1, concat_axis=0, tiled=True)
    qg = lax.all_to_all(pack(queries, grad_context), "ctx", split_axis=1, concat_axis=0, tiled=True)
    seg_len = kv.shape[0]
    local_blocks = seg_len // BLK
    group = lax.axis_index("fsdp")
    low, high = neighbours(kv, 0, BLK)
    owner = global_blocks // local_blocks
    spot = global_blocks % local_blocks
    picks = []
    for which in range(GLOB):
        piece = lax.dynamic_slice_in_dim(kv, spot[which] * BLK, BLK, 0)
        picks.append(jnp.where(owner[which] == group, piece, jnp.zeros_like(piece)))
    shared = lax.psum(jnp.concatenate(picks, axis=0), "fsdp")
    ids, bias = tables(global_blocks, random_blocks[:, 0], local_blocks)
    dqo, sums = attend(ids, jnp.concatenate([low, kv, high, shared], axis=0), qg, bias)
    edges = jnp.concatenate([sums[:BLK], sums[BLK + seg_len : 2 * BLK + seg_len]], axis=0)
    from_low, from_high = neighbours(edges, 0, BLK)
    local = sums[BLK : BLK + seg_len]
    local = local.at[:BLK].add(from_low)
    local = local.at[seg_len - BLK :].add(from_high)
    global_sums = lax.psum(sums[2 * BLK + seg_len :], "fsdp")
    for which in range(GLOB):
        term = global_sums[which * BLK : (which + 1) * BLK]
        term = jnp.where(owner[which] == group, term, jnp.zeros_like(term))
        begin = spot[which] * BLK
        current = lax.dynamic_slice_in_dim(local, begin, BLK, 0)
        local = lax.dynamic_update_slice_in_dim(local, current + term, begin, 0)
    dkv = local.astype(jnp.bfloat16)
    grad_query, context = unpack(lax.all_to_all(dqo, "ctx", split_axis=0, concat_axis=1, tiled=True))
    grad_key, grad_value = unpack(
        lax.all_to_all(dkv, "ctx", split_axis=0, concat_axis=1, tiled=True)
    )
    return (context, grad_query, grad_key, grad_value)


def solution(mesh):
    split = P(("fsdp", "ctx"), None)
    return jax.shard_map(
        body,
        mesh=mesh,
        in_specs=(split, split, split, P("fsdp", None), split, P(), P(), P("fsdp", "ctx", None)),
        out_specs=(split, split, split, split),
        check_vma=False,
    )
```

time: 895 us -> 418 us (0.47)
  local copies, waits for them, and re-layouts: 265 us -> 19.7 us
  matrix products: 206 us -> 6.3 us
  other arithmetic: 109 us -> 10.7 us
  waiting for transfers between devices: 164 us -> 226 us
  Pallas kernels: 0 us -> 28.7 us
  blocking collectives: 53.3 us -> 43.7 us
    dot_general x81 -> x1, matrix products: 206 us -> 6.3 us  [contract(): lax.dot_general(a, b, (((da,), (db,)), ((), ())), preferred_element_type=...]
    all_gather x1, waiting for transfers between devices: 7.73 us -> 93.4 us  [body(): lax.all_gather(out_weight, 'fsdp', axis=0, tiled=True)]
    dynamic_update_slice x50 -> x0, local copies, waits for them, and re-layouts: 84 us -> none  [the longest x48 80.8 us: add_rows(): return lax.dynamic_update_slice_in_dim(total, current + rows, begin, 0)]
    add x49 -> x6, other arithmetic: 47.8 us -> 0.03 us  [the longest x2 0.01 us: tables(): current = first_block + local_ids]
    scatter-add x18 -> x0, local copies, waits for them, and re-layouts: 41 us -> none  [the longest x8 31.6 us: advance(): key_sum.at[1:block_count + 1].add(split_product(selector, far_keys))]
    reshape x32 -> x2, local copies, waits for them, and re-layouts: 37.2 us -> 0.18 us  [tables(): bias = jnp.repeat(bias.reshape(-1, 2), BLK, axis=1)]
    gather x16 -> x0, local copies, waits for them, and re-layouts: 32 us -> none  [the longest x8 16 us: advance(): value_group = value_ext[ids_part].reshape(per_step, slot_count * BLK, HD)]
    pallas_call x0 -> x1, Pallas kernels: none -> 28.7 us  [attend(): pl.pallas_call(functools.partial(attend_kernel, pairs), out_shape=(jax.Sh...]
  transfers between devices with their start and end apart: 14 -> 10, of which waited for: 8 -> 4; matrix products, arithmetic and copies ran while one was open for 4% -> 7% of each run, Pallas kernels for 0% -> 0%
where the time goes in v1:
time: 418 us; the launch traced here: 417 us
  waiting for transfers between devices  226 us (54%)
  starting transfers between devices  65.3 us (16%)
  blocking collectives  43.7 us (10%)
  Pallas kernels  28.7 us (7%)
  local copies, waits for them, and re-layouts  19.7 us (5%)
  between operations  17 us (4%)
  other arithmetic  10.7 us (3%)
  matrix products  6.3 us (2%)
    psum x1, waiting for transfers between devices, body(): global_sums = lax.psum(sums[2 * BLK + seg_len:], 'fsdp')  114 us
    all_gather x1, waiting for transfers between devices, body(): lax.all_gather(out_weight, 'fsdp', axis=0, tiled=True)  93.4 us
    psum x1, blocking collectives, body(): shared = lax.psum(jnp.concatenate(picks, axis=0), 'fsdp')  43.7 us
    pallas_call x1, Pallas kernels, attend(): pl.pallas_call(functools.partial(attend_kernel, pairs), out_shape=(jax.Sh...  28.7 us
    all_to_all x1, starting transfers between devices, body(): lax.all_to_all(dqo, 'ctx', split_axis=0, concat_axis=1, tiled=True)  21.2 us
    all_to_all x1, starting transfers between devices, body(): lax.all_to_all(dkv, 'ctx', split_axis=0, concat_axis=1, tiled=True)  18.6 us
    all_to_all x1, waiting for transfers between devices, body(): lax.all_to_all(dkv, 'ctx', split_axis=0, concat_axis=1, tiled=True)  14.8 us
    all_to_all x1, starting transfers between devices, body(): lax.all_to_all(pack(keys, values), 'ctx', split_axis=1, concat_axis=0, ti...  10.6 us
  transfers between devices with their start and end apart: 10, of which 4 were waited for; matrix products, arithmetic and copies ran while one was open for 7% of the time, Pallas kernels for 0%

profile of v1, /device:TPU:1, one launch (start us, length us, event | category | flops | bytes accessed | tf_op | source)
XLA Modules:
  0.0 417.3 jit_solution(17822311673001724452)
XLA Ops:
  7.9 1.3 copy.84
  9.2 1.3 copy.85
  10.7 1.2 copy.86
  11.9 10.6 %all-to-all-start = ((bf16[128,32,128]{0,2,1:T(8,128)(2,1)}), bf16[128,32,128]{0,2,1:T(8,128)(2,1)S(1)}, u32[]{:S(2)}, u32[]{:S(2)}) async-start(bf16[128,32,128]{0,2,1:T(8,128)(2,1)} %bitcast.2), calls=%async_computation | async-start | bytes 2097152 | tf_op jit(solution)/shard_map/all_to_all | solution.py:178
  24.2 3.7 compare_reduce_fusion
  28.0 93.4 %all-gather.2.cloned.1.call-done = bf16[2048,2048]{1,0:T(8,128)(2,1)} async-done(((bf16[128,2048]{1,0:T(8,128)(2,1)}), bf16[2048,2048]{1,0:T(8,128)(2,1)}) %all-gather.2.cloned.1.call-update) | async-done | bytes 8388624 | tf_op jit(solution)/shard_map/all_gather | solution.py:176
  121.4 6.3 %convolution_convert_fusion = bf16[128,2048]{1,0:T(8,128)(2,1)S(1)} fusion(bf16[2048,2048]{1,0:T(8,128)(2,1)} %all-gather.2.cloned.1.call-done, bf16[128,2048]{1,0:T(8,128)(2,1)S(1)} %copy-done.2, pred[128]{0:T(512)(128)(4,1)S(1)} %compare_reduce_fusion), kind=kOutput, calls=%fused_computation.1 | convolution fusion | flops 1074266112 | bytes 9437312 | tf_op jit(solution)/shard_map/dot_general | solution.py:18
  128.0 1.1 copy.90
  129.1 7.6 %all-to-all-start.1 = ((bf16[128,32,128]{0,2,1:T(8,128)(2,1)}), bf16[128,32,128]{0,2,1:T(8,128)(2,1)}, u32[]{:S(2)}, u32[]{:S(2)}) async-start(bf16[128,32,128]{0,2,1:T(8,128)(2,1)} %bitcast.11), calls=%async_computation.1 | async-start | bytes 2097152 | tf_op jit(solution)/shard_map/all_to_all | solution.py:179
  140.5 1.3 collective-permute-start
  141.8 1.3 collective-permute-start.1
  143.1 43.7 %psum.14 = bf16[128,128]{1,0:T(8,128)(2,1)S(1)} all-reduce(bf16[128,128]{1,0:T(8,128)(2,1)S(1)} %pad_maximum_fusion.3), channel_id=1, replica_groups=mesh['fsdp'=16,'ctx'=32] {'fsdp'}, use_global_device_ids=true, to_apply=%region_0.0 | all-reduce | flops 16384 | bytes 65536 | tf_op jit(solution)/shard_map/psum | solution.py:190
  187.0 1.6 copy.91
  188.6 28.7 %shard_map.111 = (bf16[4096,128]{1,0:T(8,128)(2,1)S(1)}, f32[4352,128]{1,0:T(8,128)S(1)}) custom-call(s32[64,8]{1,0:T(8,128)S(1)} %copy.96.ids_ref, bf16[4352,128]{1,0:T(8,128)(2,1)S(1)} %pad_maximum_fusion.kv_ref, bf16[4096,128]{1,0:T(8,128)(2,1)S(1)} %bitcast.39, f32[256,128]{1,0:T(8,128)S(1)} %copy.97.bias_ref), custom_call_target="tpu_custom_call" | custom-call | tf_op jit(solution)/shard_map/pallas_call | solution.py:111
  217.3 1.4 copy-done
  218.7 1.3 copy.98
  220.0 21.2 %all-to-all-start.2 = ((bf16[32,128,128]{1,2,0:T(8,128)(2,1)}), bf16[32,128,128]{1,2,0:T(8,128)(2,1)S(1)}, u32[]{:S(2)}, u32[]{:S(2)}) async-start(bf16[32,128,128]{1,2,0:T(8,128)(2,1)} %copy.98), calls=%async_computation.2 | async-start | bytes 2097152 | tf_op jit(solution)/shard_map/all_to_all | solution.py:206
  241.2 3.5 collective-permute-start.2
  245.4 1.5 slice.99
  246.9 1.3 collective-permute-start.3
  248.8 3.0 collective-permute-done.3
  251.8 1.4 fusion.7
  253.2 113.9 %all-reduce.2.cloned.1.call-done = f32[128,128]{1,0:T(8,128)} async-done(((f32[128,128]{1,0:T(8,128)}), f32[128,128]{1,0:T(8,128)}) %all-reduce.2.cloned.1.call-update) | async-done | bytes 65552 | tf_op jit(solution)/shard_map/psum | solution.py:198
  367.1 1.4 fusion.6
  368.5 1.4 fusion.4
  369.8 1.7 convert_element_type.7
  371.5 1.3 copy.99
  372.9 18.6 %all-to-all-start.3 = ((bf16[32,128,128]{1,2,0:T(8,128)(2,1)}), bf16[32,128,128]{1,2,0:T(8,128)(2,1)S(1)}, u32[]{:S(2)}, u32[]{:S(2)}) async-start(bf16[32,128,128]{1,2,0:T(8,128)(2,1)} %copy.99), calls=%async_computation.3 | async-start | bytes 2097152 | tf_op jit(solution)/shard_map/all_to_all | solution.py:208
  391.5 1.0 copy.101
  392.5 1.0 copy.100
  393.5 14.8 %all-to-all-done.3 = bf16[32,128,128]{1,2,0:T(8,128)(2,1)S(1)} async-done(((bf16[32,128,128]{1,2,0:T(8,128)(2,1)}), bf16[32,128,128]{1,2,0:T(8,128)(2,1)S(1)}, u32[]{:S(2)}, u32[]{:S(2)}) %all-to-all-start.3) | async-done | bytes 1048608 | tf_op jit(solution)/shard_map/all_to_all | solution.py:208
  408.4 1.0 copy.103
  (70 shorter events, 6.6 us)
Async XLA Ops:
  7.2 114.2 %all-gather.2.cloned.1.call-start = ((), (), s32[]{:S(2)}) async-start(), calls=%async_computation.4 | async-start | bytes 8912896 | tf_op jit(solution)/shard_map/all_gather | solution.py:176
  10.6 11.8 %copy-start.5 = (s32[64,1,3]{0,1,2:T(1,128)S(1)}, s32[64,1,3]{0,1,2:T(1,128)}, u32[]{:S(2)}) copy-start(s32[64,1,3]{0,1,2:T(1,128)} %param.19) | copy-start | bytes 2308
  10.7 11.9 %copy-start.6 = (s32[2]{0:T(128)S(1)}, s32[2]{0:T(128)}, u32[]{:S(2)}) copy-start(s32[2]{0:T(128)} %param.18) | copy-start | bytes 28
  10.7 12.5 %copy-start.3 = (bf16[128,2048]{1,0:T(8,128)(2,1)S(1)}, bf16[128,2048]{1,0:T(8,128)(2,1)}, u32[]{:S(2)}) copy-start(bf16[128,2048]{1,0:T(8,128)(2,1)} %param.12) | copy-start | bytes 1572868
  11.9 12.4 %copy-start.4 = (s32[8192]{0:T(1024)S(1)}, s32[8192]{0:T(1024)}, u32[]{:S(2)}) copy-start(s32[8192]{0:T(1024)} %param.17) | copy-start | bytes 98308
  11.9 109.5 %copy-start.2 = (bf16[128,2048]{1,0:T(8,128)(2,1)S(1)}, bf16[128,2048]{1,0:T(8,128)(2,1)}, u32[]{:S(2)}) copy-start(bf16[128,2048]{1,0:T(8,128)(2,1)} %param.16) | copy-start | bytes 1572868
  11.9 117.3 %all-to-all-start = ((bf16[128,32,128]{0,2,1:T(8,128)(2,1)}), bf16[128,32,128]{0,2,1:T(8,128)(2,1)S(1)}, u32[]{:S(2)}, u32[]{:S(2)}) async-start(bf16[128,32,128]{0,2,1:T(8,128)(2,1)} %bitcast.2), calls=%async_computation | async-start | bytes 2097152 | tf_op jit(solution)/shard_map/all_to_all | solution.py:178
  129.1 57.8 %all-to-all-start.1 = ((bf16[128,32,128]{0,2,1:T(8,128)(2,1)}), bf16[128,32,128]{0,2,1:T(8,128)(2,1)}, u32[]{:S(2)}, u32[]{:S(2)}) async-start(bf16[128,32,128]{0,2,1:T(8,128)(2,1)} %bitcast.11), calls=%async_computation.1 | async-start | bytes 2097152 | tf_op jit(solution)/shard_map/all_to_all | solution.py:179
  140.5 46.4 %collective-permute-start = (bf16[64,128]{1,0:T(8,128)(2,1)S(1)}, bf16[64,128]{1,0:T(8,128)(2,1)S(1)}, u32[]{:S(2)}, u32[]{:S(2)}) collective-permute-start(bf16[64,128]{1,0:T(8,128)(2,1)S(1)} %get-tuple-element.54), channel_id=1, source_target_pairs={{0,32},{32,64},{64,96},{96,128},{128,160},{160,192},{192,224},{224... | collective-permute-start | bytes 49160 | tf_op jit(solution)/shard_map/ppermute | solution.py:128
  141.8 45.1 %collective-permute-start.1 = (bf16[64,128]{1,0:T(8,128)(2,1)S(1)}, bf16[64,128]{1,0:T(8,128)(2,1)S(1)}, u32[]{:S(2)}, u32[]{:S(2)}) collective-permute-start(bf16[64,128]{1,0:T(8,128)(2,1)S(1)} %get-tuple-element.57), channel_id=1, source_target_pairs={{32,0},{64,32},{96,64},{128,96},{160,128},{192,160},{224,192},{256... | collective-permute-start | bytes 49160 | tf_op jit(solution)/shard_map/ppermute | solution.py:129
  217.3 1.4 copy-start
  218.7 22.5 %copy-start.1 = (f32[4352,128]{1,0:T(8,128)S(1)}, f32[4352,128]{1,0:T(8,128)}, u32[]{:S(2)}) copy-start(f32[4352,128]{1,0:T(8,128)} %copy-done) | copy-start | bytes 6684676
  220.0 152.9 %all-to-all-start.2 = ((bf16[32,128,128]{1,2,0:T(8,128)(2,1)}), bf16[32,128,128]{1,2,0:T(8,128)(2,1)S(1)}, u32[]{:S(2)}, u32[]{:S(2)}) async-start(bf16[32,128,128]{1,2,0:T(8,128)(2,1)} %copy.98), calls=%async_computation.2 | async-start | bytes 2097152 | tf_op jit(solution)/shard_map/all_to_all | solution.py:206
  241.2 125.9 %all-reduce.2.cloned.1.call-start = ((), (), s32[]{:S(2)}) async-start(), calls=%async_computation.5 | async-start | bytes 131072 | tf_op jit(solution)/shard_map/psum | solution.py:198
  241.2 6.9 %collective-permute-start.2 = (f32[64,128]{1,0:T(8,128)S(1)}, f32[64,128]{1,0:T(8,128)S(1)}, u32[]{:S(2)}, u32[]{:S(2)}) collective-permute-start(f32[64,128]{1,0:T(8,128)S(1)} %get-tuple-element.49), channel_id=1, source_target_pairs={{0,32},{32,64},{64,96},{96,128},{128,160},{160,192},{192,224},{224... | collective-permute-start | bytes 98312 | tf_op jit(solution)/shard_map/ppermute | solution.py:128
  246.9 5.0 %collective-permute-start.3 = (f32[64,128]{1,0:T(8,128)S(1)}, f32[64,128]{1,0:T(8,128)S(1)}, u32[]{:S(2)}, u32[]{:S(2)}) collective-permute-start(f32[64,128]{1,0:T(8,128)S(1)} %get-tuple-element.48), channel_id=1, source_target_pairs={{32,0},{64,32},{96,64},{128,96},{160,128},{192,160},{224,192},{256... | collective-permute-start | bytes 98312 | tf_op jit(solution)/shard_map/ppermute | solution.py:129
  372.9 35.5 %all-to-all-start.3 = ((bf16[32,128,128]{1,2,0:T(8,128)(2,1)}), bf16[32,128,128]{1,2,0:T(8,128)(2,1)S(1)}, u32[]{:S(2)}, u32[]{:S(2)}) async-start(bf16[32,128,128]{1,2,0:T(8,128)(2,1)} %copy.99), calls=%async_computation.3 | async-start | bytes 2097152 | tf_op jit(solution)/shard_map/all_to_all | solution.py:208
Sparse Core Ops, SparseCore 0:
  10.1 111.2 all-gather.1
  247.0 120.0 all-reduce.1

commit v2 on v1

--- a/solution.py
+++ b/solution.py
@@ -120,26 +120,647 @@
     )(ids, kv, qg, bias)
 
 
-def neighbours(block, dim, width):
-    count = lax.axis_size("fsdp")
-    forward = [(i, i + 1) for i in range(count - 1)]
-    backward = [(target, source) for source, target in forward]
-    last = lax.slice_in_dim(block, block.shape[dim] - width, None, axis=dim)
-    low = lax.ppermute(last, "fsdp", forward)
-    high = lax.ppermute(lax.slice_in_dim(block, 0, width, axis=dim), "fsdp", backward)
-    return low, high
-
-
-def pack(a, b):
-    heads = a.shape[1] // HD
-    both = jnp.stack([a.reshape(-1, heads, HD), b.reshape(-1, heads, HD)], axis=2)
-    return both.reshape(a.shape[0], 2 * a.shape[1])
-
-
-def unpack(both):
-    heads = both.shape[1] // (2 * HD)
-    split = both.reshape(-1, heads, 2, HD)
-    return split[:, :, 0].reshape(-1, heads * HD), split[:, :, 1].reshape(-1, heads * HD)
+CAP = 32
+MESH = pl.DeviceIdType.MESH
+
+
+def place(nz, nctx):
+    z = lax.axis_index("fsdp")
+    c = lax.axis_index("ctx")
+    return z, c
+
+
+def greet(nz, nctx):
+    z, c = place(nz, nctx)
+    barrier = pltpu.get_barrier_semaphore()
+
+    def plane(d, carry):
+        peer = lax.rem(c + d, nctx)
+        pl.semaphore_signal(barrier, inc=1, device_id=(z, peer), device_id_type=MESH)
+        return carry
+
+    def column(d, carry):
+        peer = lax.rem(z + d, nz)
+        pl.semaphore_signal(barrier, inc=1, device_id=(peer, c), device_id_type=MESH)
+        return carry
+
+    lax.fori_loop(1, nctx, plane, 0)
+    lax.fori_loop(1, nz, column, 0)
+    pl.semaphore_wait(barrier, nctx + nz - 2)
+
+
+def plane_copy(nz, nctx, d, src, dst, send, recv, incoming=False):
+    z, c = place(nz, nctx)
+    peer = lax.rem(c + d, nctx)
+    source = lax.rem(c - d + nctx, nctx) if incoming else c
+    return pltpu.make_async_remote_copy(
+        src_ref=src(peer),
+        dst_ref=dst(source),
+        send_sem=send.at[d],
+        recv_sem=recv.at[d],
+        device_id=(z, peer),
+        device_id_type=MESH,
+    )
+
+
+def column_copy(peer, src, dst, send, recv):
+    c = lax.axis_index("ctx")
+    return pltpu.make_async_remote_copy(
+        src_ref=src,
+        dst_ref=dst,
+        send_sem=send,
+        recv_sem=recv,
+        device_id=(peer, c),
+        device_id_type=MESH,
+    )
+
+
+def inner_copies(nz, nctx, side, src, buf, send, recv):
+    z, c = place(nz, nctx)
+    group, member = z // side, lax.rem(z, side)
+    return [
+        column_copy(
+            group * side + lax.rem(member + e, side), src, buf.at[e], send.at[e], recv.at[e]
+        )
+        for e in range(1, side)
+    ]
+
+
+def outer_copies(nz, nctx, side, src, buf, send, recv):
+    z, c = place(nz, nctx)
+    group, member = z // side, lax.rem(z, side)
+    groups = nz // side
+    return [
+        column_copy(
+            lax.rem(group + e, groups) * side + member, src, buf.at[e], send.at[e], recv.at[e]
+        )
+        for e in range(1, groups)
+    ]
+
+
+def edge_copies(nz, down_src, down_dst, up_src, up_dst, send, recv):
+    z = lax.axis_index("fsdp")
+    down = column_copy(jnp.maximum(z - 1, 0), down_src, down_dst, send.at[0], recv.at[0])
+    up = column_copy(jnp.minimum(z + 1, nz - 1), up_src, up_dst, send.at[1], recv.at[1])
+    return down, up
+
+
+def halves(x):
+    return jnp.concatenate([x[:, HD:], x[:, :HD]], axis=1)
+
+
+def chosen(rank_row):
+    order = lax.broadcasted_iota(jnp.int32, (CAP, rank_row.shape[1]), 0).astype(jnp.float32)
+    return jnp.where(order == rank_row, 1.0, 0.0).astype(jnp.bfloat16)
+
+
+def collect_kernel(
+    nz, nctx, glob_ref, q_ref, k_ref, v_ref, ct_ref, w_ref, pos_ref,
+    kv_ref, qg_ref, rank_ref, most_ref,
+    kv_pack, q_pack, q_all, up_own, up_all, w_all, g_all, count, g_own, g_in, g_mid, g_out,
+    kv_send, kv_recv, q_send, q_recv, up_send, up_recv, w_send, w_recv, a_send, a_recv,
+    edge_send, edge_recv, in_send, in_recv, out_send, out_recv, pair_send, pair_recv,
+):
+    z, c = place(nz, nctx)
+    chip, core = c // 2, lax.rem(c, 2)
+    rows = q_ref.shape[0]
+    wide = q_ref.shape[1]
+    side = max(s for s in range(1, nz + 1) if s * s <= nz)
+    local_blocks = nctx * rows // BLK
+    partner = 2 * chip + 1 - core
+    low = lax.broadcasted_iota(jnp.int32, (BLK, 2 * HD), 1) < HD
+    greet(nz, nctx)
+
+    piece_rows = 2 * rows // nz
+
+    def piece(ref, i):
+        return ref.at[
+            pl.ds(pl.multiple_of((i // 2) * piece_rows, piece_rows), piece_rows),
+            pl.ds(pl.multiple_of(core * (wide // 2) + lax.rem(i, 2) * (wide // 4), wide // 4), wide // 4),
+        ]
+
+    def weight_out(d):
+        i = lax.rem(z + d, nz)
+        return column_copy(i, piece(w_ref, i), piece(w_all, i), w_send.at[d], w_recv)
+
+    is_source = z == chip
+
+    @pl.when(is_source)
+    def _():
+        def go(d, carry):
+            weight_out(d).start()
+            return carry
+
+        lax.fori_loop(1, nz, go, 0)
+        w_all[...] = w_ref[...]
+
+    for t in range(nctx // 2):
+        k_two = k_ref[:, 2 * t * HD : 2 * (t + 1) * HD]
+        v_two = v_ref[:, 2 * t * HD : 2 * (t + 1) * HD]
+        kv_pack[2 * t] = jnp.concatenate([k_two[:, :HD], v_two[:, :HD]], axis=1)
+        kv_pack[2 * t + 1] = jnp.concatenate([k_two[:, HD:], v_two[:, HD:]], axis=1)
+
+    def kv_rows(source):
+        return kv_ref.at[pl.ds(pl.multiple_of(BLK + source * rows, BLK), rows)]
+
+    def kv_copy(d, incoming=False):
+        return plane_copy(nz, nctx, d, lambda p: kv_pack.at[p], kv_rows, kv_send, kv_recv, incoming)
+
+    def kv_go(d, carry):
+        kv_copy(d).start()
+        return carry
+
+    lax.fori_loop(1, nctx, kv_go, 0)
+    kv_ref[pl.ds(pl.multiple_of(BLK + c * rows, BLK), rows)] = kv_pack[c]
+
+    for t in range(nctx // 2):
+        top = q_ref[:BLK, 2 * t * HD : 2 * (t + 1) * HD]
+        bottom = q_ref[BLK:, 2 * t * HD : 2 * (t + 1) * HD]
+        q_pack[2 * t] = jnp.concatenate([top[:, :HD], bottom[:, :HD]], axis=1)
+        q_pack[2 * t + 1] = jnp.concatenate([top[:, HD:], bottom[:, HD:]], axis=1)
+
+    def q_copy(d, incoming=False):
+        return plane_copy(nz, nctx, d, lambda p: q_pack.at[p], lambda s: q_all.at[s], q_send, q_recv, incoming)
+
+    def q_go(d, carry):
+        q_copy(d).start()
+        return carry
+
+    lax.fori_loop(1, nctx, q_go, 0)
+    q_all[c] = q_pack[c]
+
+    def weight_copy(d, incoming=False):
+        peer = lax.rem(z + d, nz)
+        at = piece(w_all, lax.rem(z - d + nz, nz) if incoming else z)
+        return column_copy(peer, at, at, a_send.at[d], a_recv.at[d])
+
+    @pl.when(jnp.logical_not(is_source))
+    def _():
+        column_copy(z, piece(w_ref, z), piece(w_all, z), w_send.at[0], w_recv).wait_recv()
+
+    def weight_go(d, carry):
+        @pl.when(lax.rem(z + d, nz) != chip)
+        def _():
+            weight_copy(d).start()
+
+        return carry
+
+    lax.fori_loop(1, nz, weight_go, 0)
+
+    devices = nz * nctx
+    count[...] = jnp.zeros_like(count)
+    span = pos_ref.shape[1]
+    group_ids = lax.broadcasted_iota(jnp.int32, (devices, span), 0)
+    inside_ids = lax.broadcasted_iota(jnp.int32, (rows, span), 0)
+
+    def tally(i, carry):
+        pos = pos_ref[pl.ds(i, 1), :]
+        group = pos // rows
+        inside = pos - group * rows
+        hit = jnp.where(group_ids == group, 1.0, 0.0).astype(jnp.bfloat16)
+        spot = jnp.where(inside_ids == inside, 1.0, 0.0).astype(jnp.bfloat16)
+        count[...] += contract(hit, spot, 1, 1)
+        return carry
+
+    lax.fori_loop(0, pos_ref.shape[0], tally, 0)
+    masked = jnp.where(count[...] > 0.5, 1.0, 0.0)
+    before = lax.broadcasted_iota(jnp.int32, (rows, rows), 0) < lax.broadcasted_iota(
+        jnp.int32, (rows, rows), 1
+    )
+    rank = contract(masked.astype(jnp.bfloat16), jnp.where(before, 1.0, 0.0).astype(jnp.bfloat16), 1, 0)
+    count[...] = jnp.where(masked > 0.5, rank, -1.0)
+    most = jnp.max(jnp.max(count[...], axis=0, keepdims=True), axis=1, keepdims=True)
+    most_ref[...] = jnp.broadcast_to(most, most_ref.shape)
+    rank_ref[...] = count[pl.ds(pl.multiple_of(z * nctx, nctx), nctx), :]
+    mine = chosen(rank_ref[pl.ds(c, 1), :])
+    up_own[...] = contract(mine, ct_ref[...], 1, 0).astype(jnp.bfloat16)
+
+    def up_copy(d, incoming=False):
+        peer = lax.rem(c + 2 * d, nctx)
+        source = lax.rem(chip - d + nctx // 2, nctx // 2) if incoming else chip
+        return pltpu.make_async_remote_copy(
+            src_ref=up_own,
+            dst_ref=up_all.at[pl.ds(pl.multiple_of(source * CAP, CAP), CAP)],
+            send_sem=up_send.at[d],
+            recv_sem=up_recv.at[d],
+            device_id=(z, peer),
+            device_id_type=MESH,
+        )
+
+    def up_go(d, carry):
+        up_copy(d).start()
+        return carry
+
+    lax.fori_loop(1, nctx // 2, up_go, 0)
+    up_all[pl.ds(pl.multiple_of(chip * CAP, CAP), CAP)] = up_own[...]
+
+    def kv_in(d, carry):
+        kv_copy(d, True).wait_recv()
+        return carry
+
+    lax.fori_loop(1, nctx, kv_in, 0)
+    low_edge = kv_ref.at[pl.ds(0, BLK)]
+    high_edge = kv_ref.at[pl.ds((local_blocks + 1) * BLK, BLK)]
+    down, up = edge_copies(
+        nz, kv_ref.at[pl.ds(BLK, BLK)], high_edge, kv_ref.at[pl.ds(local_blocks * BLK, BLK)],
+        low_edge, edge_send, edge_recv,
+    )
+
+    @pl.when(z > 0)
+    def _():
+        down.start()
+
+    @pl.when(z < nz - 1)
+    def _():
+        up.start()
+
+    wanted = [glob_ref[i] - z * local_blocks for i in range(GLOB)]
+
+    def pick(b, totals):
+        block = kv_ref[pl.ds(pl.multiple_of(BLK + b * BLK, BLK), BLK), :]
+        return tuple(
+            jnp.where(jnp.full(block.shape, wanted[i] == b), block, totals[i]) for i in range(GLOB)
+        )
+
+    nothing = jnp.zeros((BLK, 2 * HD), jnp.bfloat16)
+    picked = lax.fori_loop(0, local_blocks, pick, (nothing,) * GLOB)
+    g_own[...] = jnp.concatenate(picked, axis=0)
+    stage_in = inner_copies(nz, nctx, side, g_own, g_in, in_send, in_recv)
+    for copy in stage_in:
+        copy.start()
+
+    half = pl.ds(pl.multiple_of(core * (wide // 2), wide // 2), wide // 2)
+    other_half = pl.ds(pl.multiple_of((1 - core) * (wide // 2), wide // 2), wide // 2)
+
+    def pair_copy(src, dst, i):
+        return pltpu.make_async_remote_copy(
+            src_ref=src,
+            dst_ref=dst,
+            send_sem=pair_send.at[i],
+            recv_sem=pair_recv.at[i],
+            device_id=(z, partner),
+            device_id_type=MESH,
+        )
+
+    cross_out = pair_copy(w_all.at[:, half], w_all.at[:, half], 0)
+    cross_in = pair_copy(w_all.at[:, half], w_all.at[:, other_half], 0)
+
+    @pl.when(jnp.logical_not(is_source))
+    def _():
+        def weight_in(d, carry):
+            weight_copy(d, True).wait_recv()
+            return carry
+
+        lax.fori_loop(1, nz, weight_in, 0)
+        cross_out.start()
+
+    total = g_own[...].astype(jnp.float32)
+    for e, copy in enumerate(stage_in):
+        copy.wait_recv()
+        total = total + g_in[e + 1].astype(jnp.float32)
+    g_mid[...] = total.astype(jnp.bfloat16)
+    stage_out = outer_copies(nz, nctx, side, g_mid, g_out, out_send, out_recv)
+    for copy in stage_out:
+        copy.start()
+
+    def up_in(d, carry):
+        up_copy(d, True).wait_recv()
+        return carry
+
+    lax.fori_loop(1, nctx // 2, up_in, 0)
+
+    @pl.when(jnp.logical_not(is_source))
+    def _():
+        cross_in.wait_recv()
+
+    g_all[core] = contract(up_all[...], w_all[...], 1, 1).astype(jnp.bfloat16)
+    swap_out = pair_copy(g_all.at[core], g_all.at[core], 1)
+    swap_in = pair_copy(g_all.at[core], g_all.at[1 - core], 1)
+    swap_out.start()
+
+    @pl.when(z > 0)
+    def _():
+        column_copy(jnp.maximum(z - 1, 0), low_edge, low_edge, edge_send.at[1], edge_recv.at[1]).wait_recv()
+
+    @pl.when(z == 0)
+    def _():
+        kv_ref[pl.ds(0, BLK), :] = nothing
+
+    @pl.when(z < nz - 1)
+    def _():
+        column_copy(
+            jnp.minimum(z + 1, nz - 1), high_edge, high_edge, edge_send.at[0], edge_recv.at[0]
+        ).wait_recv()
+
+    @pl.when(z == nz - 1)
+    def _():
+        kv_ref[pl.ds((local_blocks + 1) * BLK, BLK), :] = nothing
+
+    total = g_mid[...].astype(jnp.float32)
+    for e, copy in enumerate(stage_out):
+        copy.wait_recv()
+        total = total + g_out[e + 1].astype(jnp.float32)
+    kv_ref[pl.ds((local_blocks + 2) * BLK, GLOB * BLK), :] = total.astype(jnp.bfloat16)
+
+    def q_in(d, carry):
+        q_copy(d, True).wait_recv()
+        return carry
+
+    lax.fori_loop(1, nctx, q_in, 0)
+    swap_in.wait_recv()
+
+    def expand(j, carry):
+        marks = chosen(rank_ref[pl.ds(j, 1), :])
+        compact = g_all[lax.rem(j, 2), pl.ds(pl.multiple_of((j // 2) * CAP, CAP), CAP), :]
+        dense = contract(marks, compact, 0, 0).astype(jnp.bfloat16)
+        dense = jnp.where(jnp.full(dense.shape, core == 0), halves(dense), dense)
+        two = q_all[j]
+        begin = pl.multiple_of(j * rows, rows)
+        qg_ref[pl.ds(begin, BLK), :] = jnp.where(low, two, dense[:BLK])
+        qg_ref[pl.ds(begin + BLK, BLK), :] = jnp.where(low, halves(two), dense[BLK:])
+        return carry
+
+    lax.fori_loop(0, nctx, expand, 0)
+
+    def left_plane(d, carry):
+        kv_copy(d).wait_send()
+        q_copy(d).wait_send()
+        return carry
+
+    lax.fori_loop(1, nctx, left_plane, 0)
+
+    def left_up(d, carry):
+        up_copy(d).wait_send()
+        return carry
+
+    lax.fori_loop(1, nctx // 2, left_up, 0)
+
+    def left_weight(d, carry):
+        @pl.when(lax.rem(z + d, nz) != chip)
+        def _():
+            weight_copy(d).wait_send()
+
+        @pl.when(is_source)
+        def _():
+            weight_out(d).wait_send()
+
+        return carry
+
+    lax.fori_loop(1, nz, left_weight, 0)
+
+    @pl.when(z > 0)
+    def _():
+        down.wait_send()
+
+    @pl.when(z < nz - 1)
+    def _():
+        up.wait_send()
+
+    for copy in stage_in + stage_out:
+        copy.wait_send()
+
+    @pl.when(jnp.logical_not(is_source))
+    def _():
+        cross_out.wait_send()
+
+    swap_out.wait_send()
+
+
+def collect(nz, nctx, global_blocks, q, k, v, ct, w, positions):
+    rows, wide = q.shape
+    region = nctx * rows
+    side = max(s for s in range(1, nz + 1) if s * s <= nz)
+    half = jnp.bfloat16
+    dma = pltpu.SemaphoreType.DMA
+    vmem = pl.BlockSpec(memory_space=pltpu.VMEM)
+    span = 256
+    return pl.pallas_call(
+        functools.partial(collect_kernel, nz, nctx),
+        out_shape=(
+            jax.ShapeDtypeStruct((region + (2 + GLOB) * BLK, 2 * HD), half),
+            jax.ShapeDtypeStruct((region, 2 * HD), half),
+            jax.ShapeDtypeStruct((nctx, rows), jnp.float32),
+            jax.ShapeDtypeStruct((8, 128), jnp.float32),
+        ),
+        in_specs=[pl.BlockSpec(memory_space=pltpu.SMEM)] + [vmem] * 6,
+        out_specs=(vmem,) * 4,
+        scratch_shapes=[
+            pltpu.VMEM((nctx, rows, 2 * HD), half),
+            pltpu.VMEM((nctx, BLK, 2 * HD), half),
+            pltpu.VMEM((nctx, BLK, 2 * HD), half),
+            pltpu.VMEM((CAP, wide), half),
+            pltpu.VMEM((nctx // 2 * CAP, wide), half),
+            pltpu.VMEM((rows, wide), half),
+            pltpu.VMEM((2, nctx // 2 * CAP, 2 * HD), half),
+            pltpu.VMEM((nz * nctx, rows), jnp.float32),
+            pltpu.VMEM((GLOB * BLK, 2 * HD), half),
+            pltpu.VMEM((side, GLOB * BLK, 2 * HD), half),
+            pltpu.VMEM((GLOB * BLK, 2 * HD), half),
+            pltpu.VMEM((nz // side, GLOB * BLK, 2 * HD), half),
+            dma((nctx,)), dma((nctx,)), dma((nctx,)), dma((nctx,)),
+            dma((nctx // 2,)), dma((nctx // 2,)),
+            dma((nz,)), dma(()), dma((nz,)), dma((nz,)),
+            dma((2,)), dma((2,)),
+            dma((side,)), dma((side,)), dma((nz // side,)), dma((nz // side,)),
+            dma((2,)), dma((2,)),
+        ],
+        compiler_params=pltpu.CompilerParams(
+            collective_id=0, has_side_effects=True, vmem_limit_bytes=56 * 1024 * 1024
+        ),
+    )(global_blocks, q, k, v, ct, w, positions.reshape(-1, span))
+
+
+def deliver_kernel(
+    nz, nctx, glob_ref, dqo_ref, sums_ref, rank_ref,
+    o_ref, dq_ref, dk_ref, dv_ref,
+    oq_pack, oq_all, kv_pack, kv_all, compact, edge_out, edge_in, g_own, g_in, g_mid, g_out,
+    oq_send, oq_recv, kv_send, kv_recv, edge_send, edge_recv, in_send, in_recv, out_send, out_recv,
+):
+    z, c = place(nz, nctx)
+    rows = o_ref.shape[0]
+    side = max(s for s in range(1, nz + 1) if s * s <= nz)
+    local_blocks = nctx * rows // BLK
+    few = CAP // 2
+    high_begin = (local_blocks + 1) * BLK
+    greet(nz, nctx)
+    edge_out[0] = sums_ref[pl.ds(0, BLK), :]
+    edge_out[1] = sums_ref[pl.ds(high_begin, BLK), :]
+    down, up = edge_copies(
+        nz, edge_out.at[0], edge_in.at[0], edge_out.at[1], edge_in.at[1], edge_send, edge_recv
+    )
+
+    @pl.when(z > 0)
+    def _():
+        down.start()
+
+    @pl.when(z < nz - 1)
+    def _():
+        up.start()
+
+    g_own[...] = sums_ref[pl.ds(high_begin + BLK, GLOB * BLK), :].astype(jnp.bfloat16)
+    stage_in = inner_copies(nz, nctx, side, g_own, g_in, in_send, in_recv)
+    for copy in stage_in:
+        copy.start()
+
+    def shrink(j, carry):
+        both = dqo_ref[pl.ds(pl.multiple_of(j * rows, rows), rows), :]
+        oq_pack[j, pl.ds(0, BLK), :] = jnp.concatenate([both[:BLK, HD:], both[BLK:, HD:]], axis=1)
+        picked = contract(chosen(rank_ref[pl.ds(j, 1), :]), both, 1, 0).astype(jnp.bfloat16)
+        oq_pack[j, pl.ds(BLK, few), :] = jnp.concatenate([picked[:few, :HD], picked[few:, :HD]], axis=1)
+        return carry
+
+    lax.fori_loop(0, nctx, shrink, 0)
+
+    def oq_copy(d, incoming=False):
+        return plane_copy(
+            nz, nctx, d, lambda p: oq_pack.at[p], lambda s: oq_all.at[s], oq_send, oq_recv, incoming
+        )
+
+    def oq_go(d, carry):
+        oq_copy(d).start()
+        return carry
+
+    lax.fori_loop(1, nctx, oq_go, 0)
+    oq_all[c] = oq_pack[c]
+
+    total = g_own[...].astype(jnp.float32)
+    for e, copy in enumerate(stage_in):
+        copy.wait_recv()
+        total = total + g_in[e + 1].astype(jnp.float32)
+    g_mid[...] = total.astype(jnp.bfloat16)
+    stage_out = outer_copies(nz, nctx, side, g_mid, g_out, out_send, out_recv)
+    for copy in stage_out:
+        copy.start()
+
+    @pl.when(z > 0)
+    def _():
+        column_copy(
+            jnp.maximum(z - 1, 0), edge_out.at[1], edge_in.at[1], edge_send.at[1], edge_recv.at[1]
+        ).wait_recv()
+
+    @pl.when(z == 0)
+    def _():
+        edge_in[1] = jnp.zeros_like(edge_in[1])
+
+    @pl.when(z < nz - 1)
+    def _():
+        column_copy(
+            jnp.minimum(z + 1, nz - 1), edge_out.at[0], edge_in.at[0], edge_send.at[0], edge_recv.at[0]
+        ).wait_recv()
+
+    @pl.when(z == nz - 1)
+    def _():
+        edge_in[0] = jnp.zeros_like(edge_in[0])
+
+    for copy in stage_out:
+        copy.wait_recv()
+    for e in range(1, nz // side):
+        total = total + g_out[e].astype(jnp.float32)
+    wanted = [glob_ref[i] - z * local_blocks for i in range(GLOB)]
+
+    def settle(j, carry):
+        for side_of in range(2):
+            b = 2 * j + side_of
+            term = sums_ref[pl.ds(pl.multiple_of((b + 1) * BLK, BLK), BLK), :]
+            for i in range(GLOB):
+                extra = total[i * BLK : (i + 1) * BLK]
+                term = term + jnp.where(jnp.full(extra.shape, wanted[i] == b), extra, 0.0)
+            edge = edge_in[1 - side_of]
+            at_edge = j == (nctx - 1) * side_of
+            term = term + jnp.where(jnp.full(edge.shape, at_edge), edge, 0.0)
+            kv_pack[j, pl.ds(side_of * BLK, BLK), :] = term.astype(jnp.bfloat16)
+        return carry
+
+    lax.fori_loop(0, nctx, settle, 0)
+
+    def kv_copy(d, incoming=False):
+        return plane_copy(
+            nz, nctx, d, lambda p: kv_pack.at[p], lambda s: kv_all.at[s], kv_send, kv_recv, incoming
+        )
+
+    def kv_go(d, carry):
+        kv_copy(d).start()
+        return carry
+
+    lax.fori_loop(1, nctx, kv_go, 0)
+    kv_all[c] = kv_pack[c]
+
+    def oq_in(d, carry):
+        oq_copy(d, True).wait_recv()
+        return carry
+
+    lax.fori_loop(1, nctx, oq_in, 0)
+    for t in range(nctx // 2):
+        columns = slice(2 * t * HD, 2 * (t + 1) * HD)
+        first, second = oq_all[2 * t], oq_all[2 * t + 1]
+        o_ref[:BLK, columns] = jnp.concatenate([first[:BLK, :HD], second[:BLK, :HD]], axis=1)
+        o_ref[BLK:, columns] = jnp.concatenate([first[:BLK, HD:], second[:BLK, HD:]], axis=1)
+        compact[:few, columns] = jnp.concatenate([first[BLK:, :HD], second[BLK:, :HD]], axis=1)
+        compact[few:, columns] = jnp.concatenate([first[BLK:, HD:], second[BLK:, HD:]], axis=1)
+    marks = chosen(rank_ref[pl.ds(c, 1), :])
+    dq_ref[...] = contract(marks, compact[...], 0, 0).astype(jnp.bfloat16)
+
+    def kv_in(d, carry):
+        kv_copy(d, True).wait_recv()
+        return carry
+
+    lax.fori_loop(1, nctx, kv_in, 0)
+    for t in range(nctx // 2):
+        columns = slice(2 * t * HD, 2 * (t + 1) * HD)
+        first, second = kv_all[2 * t], kv_all[2 * t + 1]
+        dk_ref[:, columns] = jnp.concatenate([first[:, :HD], second[:, :HD]], axis=1)
+        dv_ref[:, columns] = jnp.concatenate([first[:, HD:], second[:, HD:]], axis=1)
+
+    def left_plane(d, carry):
+        oq_copy(d).wait_send()
+        kv_copy(d).wait_send()
+        return carry
+
+    lax.fori_loop(1, nctx, left_plane, 0)
+
+    @pl.when(z > 0)
+    def _():
+        down.wait_send()
+
+    @pl.when(z < nz - 1)
+    def _():
+        up.wait_send()
+
+    for copy in stage_in + stage_out:
+        copy.wait_send()
+
+
+def deliver(nz, nctx, rows, global_blocks, dqo, sums, rank):
+    side = max(s for s in range(1, nz + 1) if s * s <= nz)
+    half = jnp.bfloat16
+    dma = pltpu.SemaphoreType.DMA
+    vmem = pl.BlockSpec(memory_space=pltpu.VMEM)
+    wide = nctx * HD
+    return pl.pallas_call(
+        functools.partial(deliver_kernel, nz, nctx),
+        out_shape=(jax.ShapeDtypeStruct((rows, wide), half),) * 4,
+        in_specs=[pl.BlockSpec(memory_space=pltpu.SMEM)] + [vmem] * 3,
+        out_specs=(vmem,) * 4,
+        scratch_shapes=[
+            pltpu.VMEM((nctx, BLK + CAP // 2, 2 * HD), half),
+            pltpu.VMEM((nctx, BLK + CAP // 2, 2 * HD), half),
+            pltpu.VMEM((nctx, rows, 2 * HD), half),
+            pltpu.VMEM((nctx, rows, 2 * HD), half),
+            pltpu.VMEM((CAP, wide), half),
+            pltpu.VMEM((2, BLK, 2 * HD), jnp.float32),
+            pltpu.VMEM((2, BLK, 2 * HD), jnp.float32),
+            pltpu.VMEM((GLOB * BLK, 2 * HD), half),
+            pltpu.VMEM((side, GLOB * BLK, 2 * HD), half),
+            pltpu.VMEM((GLOB * BLK, 2 * HD), half),
+            pltpu.VMEM((nz // side, GLOB * BLK, 2 * HD), half),
+            dma((nctx,)), dma((nctx,)), dma((nctx,)), dma((nctx,)),
+            dma((2,)), dma((2,)),
+            dma((side,)), dma((side,)), dma((nz // side,)), dma((nz // side,)),
+        ],
+        compiler_params=pltpu.CompilerParams(
+            collective_id=1, has_side_effects=True, vmem_limit_bytes=56 * 1024 * 1024
+        ),
+    )(global_blocks, dqo, sums, rank)
 
 
 def tables(global_blocks, random_blocks, local_blocks):
@@ -168,45 +789,34 @@
 
 def body(queries, keys, values, out_weight, cotangent, positions, global_blocks, random_blocks):
     rows_here = queries.shape[0]
-    offset = (lax.axis_index("fsdp") * lax.axis_size("ctx") + lax.axis_index("ctx")) * rows_here
-    places = offset + jnp.arange(rows_here, dtype=jnp.int32)
-    masked = jnp.any(positions[:, None] == places[None, :], axis=0)
-    upstream = jnp.where(masked[:, None], cotangent, jnp.zeros_like(cotangent))
-    grad_context = contract(
-        upstream, lax.all_gather(out_weight, "fsdp", axis=0, tiled=True), 1, 1
-    ).astype(jnp.bfloat16)
-    kv = lax.all_to_all(pack(keys, values), "ctx", split_axis=1, concat_axis=0, tiled=True)
-    qg = lax.all_to_all(pack(queries, grad_context), "ctx", split_axis=1, concat_axis=0, tiled=True)
-    seg_len = kv.shape[0]
-    local_blocks = seg_len // BLK
-    group = lax.axis_index("fsdp")
-    low, high = neighbours(kv, 0, BLK)
-    owner = global_blocks // local_blocks
-    spot = global_blocks % local_blocks
-    picks = []
-    for which in range(GLOB):
-        piece = lax.dynamic_slice_in_dim(kv, spot[which] * BLK, BLK, 0)
-        picks.append(jnp.where(owner[which] == group, piece, jnp.zeros_like(piece)))
-    shared = lax.psum(jnp.concatenate(picks, axis=0), "fsdp")
+    nz, nctx = lax.axis_size("fsdp"), lax.axis_size("ctx")
+    local_blocks = nctx * rows_here // BLK
+    kv, qg, rank, most = collect(
+        nz, nctx, global_blocks, queries, keys, values, cotangent, out_weight, positions
+    )
+    crowded = most[0, 0] > CAP - 0.5
+
+    def dense_gradient(qg):
+        offset = (lax.axis_index("fsdp") * nctx + lax.axis_index("ctx")) * rows_here
+        places = offset + jnp.arange(rows_here, dtype=jnp.int32)
+        masked = jnp.any(positions[:, None] == places[None, :], axis=0)
+        upstream = jnp.where(masked[:, None], cotangent, jnp.zeros_like(cotangent))
+        weight = lax.all_gather(out_weight, "fsdp", axis=0, tiled=True)
+        grad = contract(upstream, weight, 1, 1).astype(jnp.bfloat16)
+        grad = lax.all_to_all(grad, "ctx", split_axis=1, concat_axis=0, tiled=True)
+        return jnp.concatenate([qg[:, :HD], grad], axis=1)
+
+    qg = lax.cond(crowded, dense_gradient, lambda qg: qg, qg)
     ids, bias = tables(global_blocks, random_blocks[:, 0], local_blocks)
-    dqo, sums = attend(ids, jnp.concatenate([low, kv, high, shared], axis=0), qg, bias)
-    edges = jnp.concatenate([sums[:BLK], sums[BLK + seg_len : 2 * BLK + seg_len]], axis=0)
-    from_low, from_high = neighbours(edges, 0, BLK)
-    local = sums[BLK : BLK + seg_len]
-    local = local.at[:BLK].add(from_low)
-    local = local.at[seg_len - BLK :].add(from_high)
-    global_sums = lax.psum(sums[2 * BLK + seg_len :], "fsdp")
-    for which in range(GLOB):
-        term = global_sums[which * BLK : (which + 1) * BLK]
-        term = jnp.where(owner[which] == group, term, jnp.zeros_like(term))
-        begin = spot[which] * BLK
-        current = lax.dynamic_slice_in_dim(local, begin, BLK, 0)
-        local = lax.dynamic_update_slice_in_dim(local, current + term, begin, 0)
-    dkv = local.astype(jnp.bfloat16)
-    grad_query, context = unpack(lax.all_to_all(dqo, "ctx", split_axis=0, concat_axis=1, tiled=True))
-    grad_key, grad_value = unpack(
-        lax.all_to_all(dkv, "ctx", split_axis=0, concat_axis=1, tiled=True)
+    dqo, sums = attend(ids, kv, qg, bias)
+    context, grad_query, grad_key, grad_value = deliver(
+        nz, nctx, rows_here, global_blocks, dqo, sums, rank
     )
+
+    def dense_query(grad_query):
+        return lax.all_to_all(dqo[:, :HD], "ctx", split_axis=0, concat_axis=1, tiled=True)
+
+    grad_query = lax.cond(crowded, dense_query, lambda grad_query: grad_query, grad_query)
     return (context, grad_query, grad_key, grad_value)
 
 

time: 418 us -> 191 us (0.46)
  waiting for transfers between devices: 226 us -> 0 us
  Pallas kernels: 28.7 us -> 163 us
  starting transfers between devices: 65.3 us -> 0 us
  blocking collectives: 43.7 us -> 0 us
  other arithmetic: 10.7 us -> 0.86 us
  local copies, waits for them, and re-layouts: 19.7 us -> 11 us
  matrix products: 6.3 us -> 0 us
    pallas_call x0 -> x2, Pallas kernels: none -> 135 us  [the longest x1 78.8 us: collect(): pl.pallas_call(functools.partial(collect_kernel, nz, nctx), out_shape=(ja...]
    psum x1 -> x0, waiting for transfers between devices: 114 us -> none  [body(): global_sums = lax.psum(sums[2 * BLK + seg_len:], 'fsdp')]
    all_gather x1 -> x0, waiting for transfers between devices: 93.4 us -> none  [body(): lax.all_gather(out_weight, 'fsdp', axis=0, tiled=True)]
    all_to_all x4 -> x0, starting transfers between devices: 57.9 us -> none  [the longest x1 21.2 us: body(): lax.all_to_all(dqo, 'ctx', split_axis=0, concat_axis=1, tiled=True)]
    psum x1 -> x0, blocking collectives: 43.7 us -> none  [body(): shared = lax.psum(jnp.concatenate(picks, axis=0), 'fsdp')]
    all_to_all x4 -> x0, waiting for transfers between devices: 14.8 us -> none  [the longest x1 14.8 us: body(): lax.all_to_all(dkv, 'ctx', split_axis=0, concat_axis=1, tiled=True)]
    ppermute x4 -> x0, starting transfers between devices: 7.36 us -> none  [the longest x2 4.78 us: neighbours(): low = lax.ppermute(last, 'fsdp', forward)]
    dot_general x1 -> x0, matrix products: 6.3 us -> none  [contract(): lax.dot_general(a, b, (((da,), (db,)), ((), ())), preferred_element_type=...]
  transfers between devices with their start and end apart: 10 -> 0, of which waited for: 4 -> 0; matrix products, arithmetic and copies ran while one was open for 7% -> 0% of each run, Pallas kernels for 0% -> 0%
where the time goes in v2:
time: 191 us; the launch traced here: 190 us
  Pallas kernels  163 us (85%)
  between operations  14.8 us (8%)
  local copies, waits for them, and re-layouts  11 us (6%)
    pallas_call x1, Pallas kernels, collect(): pl.pallas_call(functools.partial(collect_kernel, nz, nctx), out_shape=(ja...  78.8 us
    pallas_call x1, Pallas kernels, deliver(): pl.pallas_call(functools.partial(deliver_kernel, nz, nctx), out_shape=(ja...  55.9 us
    pallas_call x1, Pallas kernels, attend(): pl.pallas_call(functools.partial(attend_kernel, pairs), out_shape=(jax.Sh...  28.7 us
    unnamed x17, local copies, waits for them, and re-layouts  7.4 us

profile of v2, /device:TPU:1, one launch (start us, length us, event | category | flops | bytes accessed | tf_op | source)
XLA Modules:
  0.0 190.2 jit_solution(5915309355174001733)
XLA Ops:
  7.2 0.1 broadcast_in_dim.25
  7.3 0.7 subtract_add_fusion
  8.0 0.1 copy.81.ids_ref
  8.1 1.4 reshape.110.pos_ref
  9.4 78.8 %shard_map.111 = (bf16[4352,128]{1,0:T(8,128)(2,1)}, bf16[4096,128]{1,0:T(8,128)(2,1)S(1)}, f32[32,128]{1,0:T(8,128)}, f32[8,128]{1,0:T(8,128)}) custom-call(s32[2]{0:T(128)} %glob_ref.3, bf16[128,2048]{1,0:T(8,128)(2,1)} %q_ref.1, bf16[128,2048]{1,0:T(8,128)(2,1)} %k_ref.1, bf16[128,2048]{1,0:T(8,128)(2,1)} %v_ref.1, bf16[128,2048]{1,0:T(8,128)(2,1)} %ct_ref.1, ...), custom_call_target="tpu_custom_call" | custom-call | tf_op jit(solution)/shard_map/pallas_call | solution.py:537
  88.3 1.2 slice.9
  90.1 0.0 copy-start.5
  90.1 0.0 copy-start.4
  90.1 0.0 copy-start.1
  90.2 0.6 copy-done.5
  90.8 0.1 broadcast_in_dim.29
  90.8 0.0 copy-done.4
  90.9 0.1 and_reduce_fusion
  91.0 0.1 copy.78
  91.1 0.1 copy.79
  91.2 0.1 broadcast_in_dim.26
  91.3 0.1 concatenate.15
  91.4 0.1 copy.77
  91.6 0.1 copy.80
  91.6 0.1 reshape.111
  91.8 0.1 copy.83.bias_ref
  91.8 0.0 copy-done.1
  91.9 28.7 %shard_map.112 = (bf16[4096,128]{1,0:T(8,128)(2,1)S(1)}, f32[4352,128]{1,0:T(8,128)S(1)}) custom-call(s32[64,8]{1,0:T(8,128)S(1)} %copy.81.ids_ref, bf16[4352,128]{1,0:T(8,128)(2,1)S(1)} %copy-done.1, bf16[4096,128]{1,0:T(8,128)(2,1)S(1)} %get-tuple-element.81.qg_ref, f32[256,128]{1,0:T(8,128)S(1)} %copy.83.bias_ref), custom_call_target="tpu_custom_call" | custom-call | tf_op jit(solution)/shard_map/pallas_call | solution.py:111
  120.5 0.0 copy-start
  120.6 1.4 copy-done
  121.9 55.9 %shard_map.113 = (bf16[128,2048]{1,0:T(8,128)(2,1)}, bf16[128,2048]{1,0:T(8,128)(2,1)}, bf16[128,2048]{1,0:T(8,128)(2,1)}, bf16[128,2048]{1,0:T(8,128)(2,1)}) custom-call(s32[2]{0:T(128)} %glob_ref.3, bf16[4096,128]{1,0:T(8,128)(2,1)S(1)} %get-tuple-element.38.dqo_ref, f32[4352,128]{1,0:T(8,128)} %copy-done, f32[32,128]{1,0:T(8,128)} %get-tuple-element.40.rank_ref), custom_call_target="tpu_custom_call" | custom-call | tf_op jit(solution)/shard_map/pallas_call | solution.py:739
  177.9 0.0 copy-start.3
  177.9 0.0 copy-start.2
  177.9 2.0 %copy.110 = bf16[128,2048]{1,0:T(8,128)(2,1)} copy(bf16[128,2048]{1,0:T(8,128)(2,1)} %get-tuple-element.99) | data formatting | bytes 1048576
  179.9 1.9 copy.111
  181.7 0.8 copy.112
  182.5 0.8 copy.113
  (21 shorter events, 0.2 us)
Async XLA Ops:
  90.1 0.7 copy-start.5
  90.1 0.7 copy-start.4
  90.1 1.7 copy-start.1
  120.5 1.4 copy-start
  177.9 3.9 %copy-start.3 = (bf16[128,2048]{1,0:T(8,128)(2,1)S(1)}, bf16[128,2048]{1,0:T(8,128)(2,1)}, u32[]{:S(2)}) copy-start(bf16[128,2048]{1,0:T(8,128)(2,1)} %get-tuple-element.101) | copy-start | bytes 1572868
  177.9 4.7 %copy-start.2 = (bf16[128,2048]{1,0:T(8,128)(2,1)S(1)}, bf16[128,2048]{1,0:T(8,128)(2,1)}, u32[]{:S(2)}) copy-start(bf16[128,2048]{1,0:T(8,128)(2,1)} %get-tuple-element.102) | copy-start | bytes 1572868

commit v3 on v2

v3 whole, which is shorter than its diff:
```python
import functools
import math

import jax
import jax.numpy as jnp
from jax import lax
from jax.experimental import pallas as pl
from jax.experimental.pallas import tpu as pltpu
from jax.sharding import PartitionSpec as P

HD = 64
BLK = 64
GLOB = 2
SLOTS = 8


def contract(a, b, da, db):
    return lax.dot_general(a, b, (((da,), (db,)), ((), ())), preferred_element_type=jnp.float32)


def attend_kernel(glob_ref, pick_ref, kv_ref, qg_ref, dqo_ref, sum_ref, dkv_ref):
    width = 2 * HD
    scale = math.log2(math.e) / math.sqrt(HD)
    low = lax.broadcasted_iota(jnp.int32, (BLK, width), 1) < HD
    zero = jnp.zeros((BLK, width), jnp.bfloat16)
    dkv_ref[...] = jnp.zeros_like(dkv_ref)
    blocks = kv_ref.shape[0] // BLK
    local_blocks = qg_ref.shape[0] // BLK
    first_block = lax.axis_index("fsdp") * local_blocks
    last_block = local_blocks * lax.axis_size("fsdp") - 1
    lower = lax.broadcasted_iota(jnp.int32, (1, width), 1) < HD

    def candidates(i):
        current = first_block + i
        far = [glob_ref[g] for g in range(GLOB)] + [pick_ref[r, i] for r in range(SLOTS - 3 - GLOB)]
        usable = [current > 0, current >= 0, current < last_block]
        for n, block in enumerate(far):
            good = jnp.abs(block - current) > 1
            for earlier in far[:n]:
                good = jnp.logical_and(good, block != earlier)
            usable.append(good)
        ids = [i, i + 1, i + 2] + [blocks - GLOB + g for g in range(GLOB)]
        ids += [block - first_block + 1 for block in far[GLOB:]]
        return ids, [jnp.where(good, 0.0, -1e30) for good in usable]

    def rows(block):
        return pl.ds(pl.multiple_of(block * BLK, BLK), BLK)

    def step(j, carry):
        first = qg_ref[rows(2 * j), :]
        second = qg_ref[rows(2 * j + 1), :]
        mixed = jnp.concatenate(
            [
                jnp.concatenate([jnp.where(low, first, zero), zero], axis=1),
                jnp.concatenate([zero, jnp.where(low, second, zero)], axis=1),
                jnp.concatenate([jnp.where(low, zero, first), zero], axis=1),
                jnp.concatenate([zero, jnp.where(low, zero, second)], axis=1),
            ],
            axis=0,
        )
        left, left_bias = candidates(2 * j)
        right, right_bias = candidates(2 * j + 1)
        both = jnp.concatenate(
            [
                jnp.concatenate([kv_ref[rows(a), :], kv_ref[rows(b), :]], axis=1)
                for a, b in zip(left, right)
            ],
            axis=0,
        )
        products = contract(both, mixed, 1, 1)
        scores = []
        for s in range(SLOTS):
            part = products[s * BLK : (s + 1) * BLK, :width]
            scores.append(part * scale + jnp.where(lower, left_bias[s], right_bias[s]))
        highest = functools.reduce(jnp.maximum, scores)
        highest = jnp.max(highest, axis=0, keepdims=True)
        raised = [jnp.exp2(part - highest) for part in scores]
        total = jnp.sum(functools.reduce(jnp.add, raised), axis=0, keepdims=True)
        inverse = 1.0 / total
        probs = [part * inverse for part in raised]
        grads = [products[s * BLK : (s + 1) * BLK, width:] for s in range(SLOTS)]
        inner = functools.reduce(jnp.add, [p * g for p, g in zip(probs, grads)])
        inner = jnp.sum(inner, axis=0, keepdims=True)
        weights = jnp.concatenate(
            [
                jnp.concatenate(
                    [(p * (g - inner)).astype(jnp.bfloat16), p.astype(jnp.bfloat16)], axis=1
                )
                for p, g in zip(probs, grads)
            ],
            axis=0,
        )
        sums = contract(weights, both, 0, 0)
        eighth = jnp.where(low, 1.0 / math.sqrt(HD), 1.0)
        out_first = jnp.where(low, sums[:BLK, :width], sums[2 * BLK : 3 * BLK, :width]) * eighth
        out_second = jnp.where(low, sums[BLK : 2 * BLK, width:], sums[3 * BLK :, width:]) * eighth
        dqo_ref[rows(2 * j), :] = out_first.astype(jnp.bfloat16)
        dqo_ref[rows(2 * j + 1), :] = out_second.astype(jnp.bfloat16)
        terms = contract(weights, mixed, 1, 0)

        def term(s, side):
            return terms[s * BLK : (s + 1) * BLK, side * width : (side + 1) * width]

        dkv_ref[rows(2 * j), :] += term(0, 0)
        dkv_ref[rows(2 * j + 1), :] += term(1, 0) + term(0, 1)
        dkv_ref[rows(2 * j + 2), :] += term(2, 0) + term(1, 1)
        dkv_ref[rows(2 * j + 3), :] += term(2, 1)
        for s in range(3, 3 + GLOB):
            dkv_ref[rows(blocks - GLOB + s - 3), :] += term(s, 0) + term(s, 1)
        for s in range(3 + GLOB, SLOTS):
            dkv_ref[rows(left[s]), :] += term(s, 0)
            dkv_ref[rows(right[s]), :] += term(s, 1)
        return carry

    lax.fori_loop(0, local_blocks // 2, step, 0, unroll=2)
    eighth = jnp.where(low, 1.0 / math.sqrt(HD), 1.0)

    def finish(b, carry):
        sum_ref[rows(b), :] = (dkv_ref[rows(b), :] * eighth).astype(jnp.bfloat16)
        return carry

    lax.fori_loop(0, blocks, finish, 0, unroll=4)


def attend(global_blocks, picks, kv, qg):
    smem, vmem = pl.BlockSpec(memory_space=pltpu.SMEM), pl.BlockSpec(memory_space=pltpu.VMEM)
    return pl.pallas_call(
        attend_kernel,
        out_shape=(
            jax.ShapeDtypeStruct(qg.shape, jnp.bfloat16),
            jax.ShapeDtypeStruct(kv.shape, jnp.bfloat16),
        ),
        in_specs=[smem, smem, vmem, vmem],
        out_specs=(vmem, vmem),
        scratch_shapes=[pltpu.VMEM(kv.shape, jnp.float32)],
        compiler_params=pltpu.CompilerParams(vmem_limit_bytes=48 * 1024 * 1024),
        name="attend",
    )(global_blocks, picks, kv, qg)


CAP = 32
MESH = pl.DeviceIdType.MESH


def place(nz, nctx):
    z = lax.axis_index("fsdp")
    c = lax.axis_index("ctx")
    return z, c


def greet(nz, nctx):
    z, c = place(nz, nctx)
    barrier = pltpu.get_barrier_semaphore()

    def plane(d, carry):
        peer = lax.rem(c + d, nctx)
        pl.semaphore_signal(barrier, inc=1, device_id=(z, peer), device_id_type=MESH)
        return carry

    def column(d, carry):
        peer = lax.rem(z + d, nz)
        pl.semaphore_signal(barrier, inc=1, device_id=(peer, c), device_id_type=MESH)
        return carry

    lax.fori_loop(1, nctx, plane, 0)
    lax.fori_loop(1, nz, column, 0)


def meet(nz, nctx):
    pl.semaphore_wait(pltpu.get_barrier_semaphore(), nctx + nz - 2)


def plane_copy(nz, nctx, d, src, dst, send, recv):
    z, c = place(nz, nctx)
    peer = lax.rem(c + d, nctx)
    return pltpu.make_async_remote_copy(
        src_ref=src(peer),
        dst_ref=dst(c),
        send_sem=send,
        recv_sem=recv,
        device_id=(z, peer),
        device_id_type=MESH,
    )


def all_of(view, send, recv):
    z, c = lax.axis_index("fsdp"), lax.axis_index("ctx")
    return pltpu.make_async_remote_copy(
        src_ref=view,
        dst_ref=view,
        send_sem=send,
        recv_sem=recv,
        device_id=(z, lax.bitwise_xor(c, 1)),
        device_id_type=MESH,
    )


def column_copy(peer, src, dst, send, recv):
    c = lax.axis_index("ctx")
    return pltpu.make_async_remote_copy(
        src_ref=src,
        dst_ref=dst,
        send_sem=send,
        recv_sem=recv,
        device_id=(peer, c),
        device_id_type=MESH,
    )


def inner_copies(nz, nctx, side, src, buf, send, recv):
    z, c = place(nz, nctx)
    group, member = z // side, lax.rem(z, side)
    return [
        column_copy(
            group * side + lax.rem(member + e, side), src, buf.at[e], send.at[e], recv.at[e]
        )
        for e in range(1, side)
    ]


def outer_copies(nz, nctx, side, src, buf, send, recv):
    z, c = place(nz, nctx)
    group, member = z // side, lax.rem(z, side)
    groups = nz // side
    return [
        column_copy(
            lax.rem(group + e, groups) * side + member, src, buf.at[e], send.at[e], recv.at[e]
        )
        for e in range(1, groups)
    ]


def edge_copies(nz, down_src, down_dst, up_src, up_dst, send, recv):
    z = lax.axis_index("fsdp")
    down = column_copy(jnp.maximum(z - 1, 0), down_src, down_dst, send.at[0], recv.at[0])
    up = column_copy(jnp.minimum(z + 1, nz - 1), up_src, up_dst, send.at[1], recv.at[1])
    return down, up


def halves(x):
    return jnp.concatenate([x[:, HD:], x[:, :HD]], axis=1)


def chosen(rank_row):
    order = lax.broadcasted_iota(jnp.int32, (CAP, rank_row.shape[1]), 0).astype(jnp.float32)
    return jnp.where(order == rank_row, 1.0, 0.0).astype(jnp.bfloat16)


def square(n):
    return max(s for s in range(1, n + 1) if s * s <= n)


def collect_kernel(
    nz, nctx, glob_ref, q_ref, k_ref, v_ref, ct_ref, w_ref, pos_ref,
    kv_ref, qg_ref, rank_ref, most_ref,
    kv_pack, q_pack, q_all, up_own, up_all, w_all, p_out, p_in, g_all, count, g_own, g_in, g_mid, g_out,
    kv_send, kv_recv, q_send, q_recv, up_send, up_recv, w_send, w_recv, a_send, a_recv, p_send, p_recv,
    edge_send, edge_recv, in_send, in_recv, out_send, out_recv, pair_send, pair_recv, own_sem,
):
    z, c = place(nz, nctx)
    chip, core = c // 2, lax.rem(c, 2)
    cuts = square(nctx // 2)
    x, y = chip // cuts, lax.rem(chip, cuts)
    rows = q_ref.shape[0]
    wide = q_ref.shape[1]
    depth = wide // cuts
    side = square(nz)
    local_blocks = nctx * rows // BLK
    partner = 2 * chip + 1 - core
    low = lax.broadcasted_iota(jnp.int32, (BLK, 2 * HD), 1) < HD
    greet(nz, nctx)

    for t in range(nctx // 2):
        columns = slice(2 * t * HD, 2 * (t + 1) * HD)
        k_two, v_two = k_ref[:, columns], v_ref[:, columns]
        kv_pack[2 * t] = jnp.concatenate([k_two[:, :HD], v_two[:, :HD]], axis=1)
        kv_pack[2 * t + 1] = jnp.concatenate([k_two[:, HD:], v_two[:, HD:]], axis=1)
    meet(nz, nctx)

    def kv_copy(d):
        return plane_copy(
            nz, nctx, d, lambda p: kv_pack.at[p],
            lambda s: kv_ref.at[pl.ds(pl.multiple_of(BLK + s * rows, BLK), rows)], kv_send, kv_recv,
        )

    def kv_go(d, carry):
        kv_copy(d).start()
        return carry

    column_parts = max(1, depth // 256)
    piece_rows = rows * column_parts // nz

    def piece_at(i, begin):
        return (
            pl.ds(pl.multiple_of((i // column_parts) * piece_rows, piece_rows), piece_rows),
            pl.ds(
                pl.multiple_of(
                    begin + core * (depth // 2) + lax.rem(i, column_parts) * 128, 128
                ),
                128,
            ),
        )

    def weight_out(d):
        i = lax.rem(z + d, nz)
        return column_copy(
            i, w_ref.at[piece_at(i, x * depth)], w_all.at[(z // cuts,) + piece_at(i, 0)],
            w_send.at[d], w_recv.at[z // cuts],
        )

    own_piece = pltpu.make_async_copy(
        w_ref.at[piece_at(z, x * depth)], w_all.at[(z // cuts,) + piece_at(z, 0)], own_sem
    )
    is_source = lax.rem(z, cuts) == y

    @pl.when(is_source)
    def _():
        def go(d, carry):
            weight_out(d).start()
            return carry

        lax.fori_loop(1, nz, go, 0)
        own_piece.start()

    lax.fori_loop(1, nctx, kv_go, 0)
    kv_ref[pl.ds(pl.multiple_of(BLK + c * rows, BLK), rows)] = kv_pack[c]

    for t in range(nctx // 2):
        columns = slice(2 * t * HD, 2 * (t + 1) * HD)
        top, bottom = q_ref[:BLK, columns], q_ref[BLK:, columns]
        q_pack[2 * t] = jnp.concatenate([top[:, :HD], bottom[:, :HD]], axis=1)
        q_pack[2 * t + 1] = jnp.concatenate([top[:, HD:], bottom[:, HD:]], axis=1)

    for s in range(cuts):

        @pl.when(z != s * cuts + y)
        def _():
            column_copy(
                lax.rem(z + 1, nz), w_ref.at[piece_at(z, x * depth)], w_all.at[(s,) + piece_at(z, 0)],
                w_send.at[0], w_recv.at[s],
            ).wait_recv()

    @pl.when(is_source)
    def _():
        own_piece.wait()

    def weight_copy(d, incoming=False):
        at = w_all.at[
            (slice(None),) + piece_at(lax.rem(z - d + nz, nz) if incoming else z, 0)
        ]
        return column_copy(lax.rem(z + d, nz), at, at, a_send.at[d], a_recv.at[d])

    def weight_go(d, carry):
        weight_copy(d).start()
        return carry

    lax.fori_loop(1, nz, weight_go, 0)

    devices = nz * nctx
    count[...] = jnp.zeros_like(count)
    span = 2 * pos_ref.shape[1]
    group_ids = lax.broadcasted_iota(jnp.int32, (devices, span), 0)
    inside_ids = lax.broadcasted_iota(jnp.int32, (rows, span), 0)

    def tally(i, carry):
        pos = jnp.concatenate([pos_ref[pl.ds(2 * i, 1), :], pos_ref[pl.ds(2 * i + 1, 1), :]], axis=1)
        group = pos // rows
        inside = pos - group * rows
        hit = jnp.where(group_ids == group, 1.0, 0.0).astype(jnp.bfloat16)
        spot = jnp.where(inside_ids == inside, 1.0, 0.0).astype(jnp.bfloat16)
        count[...] += contract(hit, spot, 1, 1)
        return carry

    lax.fori_loop(0, pos_ref.shape[0] // 2, tally, 0)
    masked = jnp.where(count[...] > 0.5, 1.0, 0.0)
    before = lax.broadcasted_iota(jnp.int32, (rows, rows), 0) < lax.broadcasted_iota(
        jnp.int32, (rows, rows), 1
    )
    rank = contract(masked.astype(jnp.bfloat16), jnp.where(before, 1.0, 0.0).astype(jnp.bfloat16), 1, 0)
    count[...] = jnp.where(masked > 0.5, rank, -1.0)
    most = jnp.max(jnp.max(count[...], axis=0, keepdims=True), axis=1, keepdims=True)
    most_ref[...] = jnp.broadcast_to(most, most_ref.shape)
    rank_ref[...] = count[pl.ds(pl.multiple_of(z * nctx, nctx), nctx), :]
    mine = chosen(rank_ref[pl.ds(c, 1), :])
    up_own[...] = contract(mine, ct_ref[...], 1, 0).astype(jnp.bfloat16)

    def share(i):
        return pl.ds(pl.multiple_of(i * depth, depth), depth)

    def up_copy(d):
        target = lax.rem(chip + d, nctx // 2)
        return pltpu.make_async_remote_copy(
            src_ref=up_own.at[:, share(target // cuts)],
            dst_ref=up_all.at[pl.ds(pl.multiple_of(chip * CAP, CAP), CAP)],
            send_sem=up_send,
            recv_sem=up_recv,
            device_id=(z, 2 * target + core),
            device_id_type=MESH,
        )

    def up_go(d, carry):
        up_copy(d).start()
        return carry

    lax.fori_loop(1, nctx // 2, up_go, 0)
    up_all[pl.ds(pl.multiple_of(chip * CAP, CAP), CAP)] = up_own[:, share(x)]

    def q_go(d, carry):
        plane_copy(
            nz, nctx, d, lambda p: q_pack.at[p], lambda s: q_all.at[s], q_send, q_recv
        ).start()
        return carry

    lax.fori_loop(1, nctx, q_go, 0)
    q_all[c] = q_pack[c]

    all_of(kv_ref.at[pl.ds(0, (nctx - 1) * rows)], kv_send, kv_recv).wait_recv()
    low_edge = kv_ref.at[pl.ds(0, BLK)]
    high_edge = kv_ref.at[pl.ds((local_blocks + 1) * BLK, BLK)]
    down, up = edge_copies(
        nz, kv_ref.at[pl.ds(BLK, BLK)], high_edge, kv_ref.at[pl.ds(local_blocks * BLK, BLK)],
        low_edge, edge_send, edge_recv,
    )
    wanted = [glob_ref[i] - z * local_blocks for i in range(GLOB)]

    def pick(b, totals):
        block = kv_ref[pl.ds(pl.multiple_of(BLK + b * BLK, BLK), BLK), :]
        return tuple(
            jnp.where(jnp.full(block.shape, wanted[i] == b), block, totals[i]) for i in range(GLOB)
        )

    nothing = jnp.zeros((BLK, 2 * HD), jnp.bfloat16)
    picked = lax.fori_loop(0, local_blocks, pick, (nothing,) * GLOB, unroll=8)
    g_own[...] = jnp.concatenate(picked, axis=0)
    stage_in = inner_copies(nz, nctx, side, g_own, g_in, in_send, in_recv)
    for copy in stage_in:
        copy.start()

    @pl.when(z > 0)
    def _():
        down.start()

    @pl.when(z < nz - 1)
    def _():
        up.start()

    half = pl.ds(pl.multiple_of(core * (depth // 2), depth // 2), depth // 2)
    other_half = pl.ds(pl.multiple_of((1 - core) * (depth // 2), depth // 2), depth // 2)

    def pair_copy(src, dst, i):
        return pltpu.make_async_remote_copy(
            src_ref=src,
            dst_ref=dst,
            send_sem=pair_send.at[i],
            recv_sem=pair_recv.at[i],
            device_id=(z, partner),
            device_id_type=MESH,
        )

    cross_out = pair_copy(w_all.at[:, :, half], w_all.at[:, :, half], 0)
    cross_in = pair_copy(w_all.at[:, :, other_half], w_all.at[:, :, other_half], 0)

    def weight_in(d, carry):
        weight_copy(d, True).wait_recv()
        return carry

    lax.fori_loop(1, nz, weight_in, 0)
    cross_out.start()

    total = g_own[...].astype(jnp.float32)
    for e, copy in enumerate(stage_in):
        copy.wait_recv()
        total = total + g_in[e + 1].astype(jnp.float32)
    g_mid[...] = total.astype(jnp.bfloat16)
    stage_out = outer_copies(nz, nctx, side, g_mid, g_out, out_send, out_recv)
    for copy in stage_out:
        copy.start()

    all_of(up_all.at[pl.ds(0, (nctx // 2 - 1) * CAP)], up_send, up_recv).wait_recv()
    cross_in.wait_recv()
    for s in range(cuts):
        p_out[s] = contract(up_all[...], w_all[s], 1, 1)

    def partial_copy(e):
        target = lax.rem(x + e, cuts)
        return pltpu.make_async_remote_copy(
            src_ref=p_out.at[target],
            dst_ref=p_in.at[e],
            send_sem=p_send.at[e],
            recv_sem=p_recv.at[e],
            device_id=(z, 2 * (target * cuts + y) + core),
            device_id_type=MESH,
        )

    partials = [partial_copy(e) for e in range(1, cuts)]
    for copy in partials:
        copy.start()

    @pl.when(z > 0)
    def _():
        column_copy(jnp.maximum(z - 1, 0), low_edge, low_edge, edge_send.at[1], edge_recv.at[1]).wait_recv()

    @pl.when(z == 0)
    def _():
        kv_ref[pl.ds(0, BLK), :] = nothing

    @pl.when(z < nz - 1)
    def _():
        column_copy(
            jnp.minimum(z + 1, nz - 1), high_edge, high_edge, edge_send.at[0], edge_recv.at[0]
        ).wait_recv()

    @pl.when(z == nz - 1)
    def _():
        kv_ref[pl.ds((local_blocks + 1) * BLK, BLK), :] = nothing

    total = g_mid[...].astype(jnp.float32)
    for e, copy in enumerate(stage_out):
        copy.wait_recv()
        total = total + g_out[e + 1].astype(jnp.float32)
    kv_ref[pl.ds((local_blocks + 2) * BLK, GLOB * BLK), :] = total.astype(jnp.bfloat16)

    grad = p_out[x]
    for e, copy in enumerate(partials):
        copy.wait_recv()
        grad = grad + p_in[e + 1]
    g_all[core] = grad.astype(jnp.bfloat16)
    swap_out = pair_copy(g_all.at[core], g_all.at[core], 1)
    swap_in = pair_copy(g_all.at[1 - core], g_all.at[1 - core], 1)
    swap_out.start()
    all_of(q_all.at[pl.ds(0, nctx - 1)], q_send, q_recv).wait_recv()
    swap_in.wait_recv()

    def expand(j, carry):
        marks = chosen(rank_ref[pl.ds(j, 1), :])
        compact = g_all[lax.rem(j, 2), pl.ds(pl.multiple_of((j // 2) * CAP, CAP), CAP), :]
        dense = contract(marks, compact, 0, 0).astype(jnp.bfloat16)
        dense = jnp.where(jnp.full(dense.shape, core == 0), halves(dense), dense)
        two = q_all[j]
        begin = pl.multiple_of(j * rows, rows)
        qg_ref[pl.ds(begin, BLK), :] = jnp.where(low, two, dense[:BLK])
        qg_ref[pl.ds(begin + BLK, BLK), :] = jnp.where(low, halves(two), dense[BLK:])
        return carry

    lax.fori_loop(0, nctx, expand, 0, unroll=4)

    all_of(kv_pack.at[pl.ds(0, nctx - 1)], kv_send, kv_recv).wait_send()
    all_of(q_pack.at[pl.ds(0, nctx - 1)], q_send, q_recv).wait_send()
    all_of(up_all.at[pl.ds(0, (nctx // 2 - 1) * CAP)], up_send, up_recv).wait_send()

    def left_weight(d, carry):
        weight_copy(d).wait_send()

        @pl.when(is_source)
        def _():
            weight_out(d).wait_send()

        return carry

    lax.fori_loop(1, nz, left_weight, 0)

    @pl.when(z > 0)
    def _():
        down.wait_send()

    @pl.when(z < nz - 1)
    def _():
        up.wait_send()

    for copy in stage_in + stage_out + partials:
        copy.wait_send()
    cross_out.wait_send()
    swap_out.wait_send()


def collect(nz, nctx, global_blocks, q, k, v, ct, w, positions):
    rows, wide = q.shape
    region = nctx * rows
    side, cuts = square(nz), square(nctx // 2)
    half = jnp.bfloat16
    dma = pltpu.SemaphoreType.DMA
    vmem = pl.BlockSpec(memory_space=pltpu.VMEM)
    return pl.pallas_call(
        functools.partial(collect_kernel, nz, nctx),
        out_shape=(
            jax.ShapeDtypeStruct((region + (2 + GLOB) * BLK, 2 * HD), half),
            jax.ShapeDtypeStruct((region, 2 * HD), half),
            jax.ShapeDtypeStruct((nctx, rows), jnp.float32),
            jax.ShapeDtypeStruct((8, 128), jnp.float32),
        ),
        in_specs=[pl.BlockSpec(memory_space=pltpu.SMEM)] + [vmem] * 6,
        out_specs=(vmem,) * 4,
        scratch_shapes=[
            pltpu.VMEM((nctx, rows, 2 * HD), half),
            pltpu.VMEM((nctx, BLK, 2 * HD), half),
            pltpu.VMEM((nctx, BLK, 2 * HD), half),
            pltpu.VMEM((CAP, wide), half),
            pltpu.VMEM((nctx // 2 * CAP, wide // cuts), half),
            pltpu.VMEM((cuts, rows, wide // cuts), half),
            pltpu.VMEM((cuts, nctx // 2 * CAP, 2 * HD), jnp.float32),
            pltpu.VMEM((cuts, nctx // 2 * CAP, 2 * HD), jnp.float32),
            pltpu.VMEM((2, nctx // 2 * CAP, 2 * HD), half),
            pltpu.VMEM((nz * nctx, rows), jnp.float32),
            pltpu.VMEM((GLOB * BLK, 2 * HD), half),
            pltpu.VMEM((side, GLOB * BLK, 2 * HD), half),
            pltpu.VMEM((GLOB * BLK, 2 * HD), half),
            pltpu.VMEM((nz // side, GLOB * BLK, 2 * HD), half),
            dma(()), dma(()), dma(()), dma(()), dma(()), dma(()),
            dma((nz,)), dma((cuts,)), dma((nz,)), dma((nz,)), dma((cuts,)), dma((cuts,)),
            dma((2,)), dma((2,)),
            dma((side,)), dma((side,)), dma((nz // side,)), dma((nz // side,)),
            dma((2,)), dma((2,)), dma(()),
        ],
        compiler_params=pltpu.CompilerParams(
            collective_id=0, has_side_effects=True, vmem_limit_bytes=56 * 1024 * 1024
        ),
        name="collect",
    )(global_blocks, q, k, v, ct, w, positions.reshape(-1, 128))


def deliver_kernel(
    nz, nctx, glob_ref, dqo_ref, sums_ref, rank_ref,
    oq_all, kv_all,
    oq_pack, kv_pack, edge_out, edge_in, g_own, g_in, g_mid, g_out,
    oq_send, oq_recv, kv_send, kv_recv, edge_send, edge_recv, in_send, in_recv, out_send, out_recv,
):
    z, c = place(nz, nctx)
    rows = kv_all.shape[1]
    side = square(nz)
    local_blocks = nctx * rows // BLK
    few = CAP // 2
    high_begin = (local_blocks + 1) * BLK
    greet(nz, nctx)
    edge_out[0] = sums_ref[pl.ds(0, BLK), :]
    edge_out[1] = sums_ref[pl.ds(high_begin, BLK), :]
    g_own[...] = sums_ref[pl.ds(high_begin + BLK, GLOB * BLK), :]

    def shrink(j, carry):
        both = dqo_ref[pl.ds(pl.multiple_of(j * rows, rows), rows), :]
        oq_pack[j, pl.ds(0, BLK), :] = jnp.concatenate([both[:BLK, HD:], both[BLK:, HD:]], axis=1)
        picked = contract(chosen(rank_ref[pl.ds(j, 1), :]), both, 1, 0).astype(jnp.bfloat16)
        oq_pack[j, pl.ds(BLK, few), :] = jnp.concatenate([picked[:few, :HD], picked[few:, :HD]], axis=1)
        return carry

    lax.fori_loop(0, nctx, shrink, 0, unroll=4)
    meet(nz, nctx)
    stage_in = inner_copies(nz, nctx, side, g_own, g_in, in_send, in_recv)
    for copy in stage_in:
        copy.start()
    down, up = edge_copies(
        nz, edge_out.at[0], edge_in.at[0], edge_out.at[1], edge_in.at[1], edge_send, edge_recv
    )

    @pl.when(z > 0)
    def _():
        down.start()

    @pl.when(z < nz - 1)
    def _():
        up.start()

    def oq_go(d, carry):
        plane_copy(
            nz, nctx, d, lambda p: oq_pack.at[p], lambda s: oq_all.at[s], oq_send, oq_recv
        ).start()
        return carry

    lax.fori_loop(1, nctx, oq_go, 0)
    oq_all[c] = oq_pack[c]

    total = g_own[...].astype(jnp.float32)
    for e, copy in enumerate(stage_in):
        copy.wait_recv()
        total = total + g_in[e + 1].astype(jnp.float32)
    g_mid[...] = total.astype(jnp.bfloat16)
    stage_out = outer_copies(nz, nctx, side, g_mid, g_out, out_send, out_recv)
    for copy in stage_out:
        copy.start()

    @pl.when(z > 0)
    def _():
        column_copy(
            jnp.maximum(z - 1, 0), edge_out.at[1], edge_in.at[1], edge_send.at[1], edge_recv.at[1]
        ).wait_recv()

    @pl.when(z == 0)
    def _():
        edge_in[1] = jnp.zeros_like(edge_in[1])

    @pl.when(z < nz - 1)
    def _():
        column_copy(
            jnp.minimum(z + 1, nz - 1), edge_out.at[0], edge_in.at[0], edge_send.at[0], edge_recv.at[0]
        ).wait_recv()

    @pl.when(z == nz - 1)
    def _():
        edge_in[0] = jnp.zeros_like(edge_in[0])

    for copy in stage_out:
        copy.wait_recv()
    for e in range(1, nz // side):
        total = total + g_out[e].astype(jnp.float32)
    wanted = [glob_ref[i] - z * local_blocks for i in range(GLOB)]

    def settle(j, carry):
        for side_of in range(2):
            b = 2 * j + side_of
            term = sums_ref[pl.ds(pl.multiple_of((b + 1) * BLK, BLK), BLK), :].astype(jnp.float32)
            for i in range(GLOB):
                extra = total[i * BLK : (i + 1) * BLK]
                term = term + jnp.where(jnp.full(extra.shape, wanted[i] == b), extra, 0.0)
            edge = edge_in[1 - side_of].astype(jnp.float32)
            at_edge = j == (nctx - 1) * side_of
            term = term + jnp.where(jnp.full(edge.shape, at_edge), edge, 0.0)
            kv_pack[j, pl.ds(side_of * BLK, BLK), :] = term.astype(jnp.bfloat16)
        return carry

    lax.fori_loop(0, nctx, settle, 0, unroll=2)

    def kv_go(d, carry):
        plane_copy(
            nz, nctx, d, lambda p: kv_pack.at[p], lambda s: kv_all.at[s], kv_send, kv_recv
        ).start()
        return carry

    lax.fori_loop(1, nctx, kv_go, 0)
    kv_all[c] = kv_pack[c]

    all_of(oq_all.at[pl.ds(0, nctx - 1)], oq_send, oq_recv).wait_recv()
    all_of(kv_all.at[pl.ds(0, nctx - 1)], kv_send, kv_recv).wait_recv()
    all_of(oq_pack.at[pl.ds(0, nctx - 1)], oq_send, oq_recv).wait_send()
    all_of(kv_pack.at[pl.ds(0, nctx - 1)], kv_send, kv_recv).wait_send()

    @pl.when(z > 0)
    def _():
        down.wait_send()

    @pl.when(z < nz - 1)
    def _():
        up.wait_send()

    for copy in stage_in + stage_out:
        copy.wait_send()


def deliver(nz, nctx, rows, global_blocks, dqo, sums, rank):
    side = square(nz)
    half = jnp.bfloat16
    dma = pltpu.SemaphoreType.DMA
    vmem = pl.BlockSpec(memory_space=pltpu.VMEM)
    return pl.pallas_call(
        functools.partial(deliver_kernel, nz, nctx),
        out_shape=(
            jax.ShapeDtypeStruct((nctx, BLK + CAP // 2, 2 * HD), half),
            jax.ShapeDtypeStruct((nctx, rows, 2 * HD), half),
        ),
        in_specs=[pl.BlockSpec(memory_space=pltpu.SMEM)] + [vmem] * 3,
        out_specs=(vmem,) * 2,
        scratch_shapes=[
            pltpu.VMEM((nctx, BLK + CAP // 2, 2 * HD), half),
            pltpu.VMEM((nctx, rows, 2 * HD), half),
            pltpu.VMEM((2, BLK, 2 * HD), half),
            pltpu.VMEM((2, BLK, 2 * HD), half),
            pltpu.VMEM((GLOB * BLK, 2 * HD), half),
            pltpu.VMEM((side, GLOB * BLK, 2 * HD), half),
            pltpu.VMEM((GLOB * BLK, 2 * HD), half),
            pltpu.VMEM((nz // side, GLOB * BLK, 2 * HD), half),
            dma(()), dma(()), dma(()), dma(()),
            dma((2,)), dma((2,)),
            dma((side,)), dma((side,)), dma((nz // side,)), dma((nz // side,)),
        ],
        compiler_params=pltpu.CompilerParams(
            collective_id=1, has_side_effects=True, vmem_limit_bytes=56 * 1024 * 1024
        ),
        name="deliver",
    )(global_blocks, dqo, sums, rank)


def spread_kernel(oq_ref, kv_ref, rank_ref, most_ref, full_ref, o_ref, dq_ref, dk_ref, dv_ref, compact):
    few = CAP // 2
    for t in range(oq_ref.shape[0] // 2):
        columns = slice(2 * t * HD, 2 * (t + 1) * HD)
        first, second = oq_ref[2 * t], oq_ref[2 * t + 1]
        o_ref[:BLK, columns] = jnp.concatenate([first[:BLK, :HD], second[:BLK, :HD]], axis=1)
        o_ref[BLK:, columns] = jnp.concatenate([first[:BLK, HD:], second[:BLK, HD:]], axis=1)
        compact[:few, columns] = jnp.concatenate([first[BLK:, :HD], second[BLK:, :HD]], axis=1)
        compact[few:, columns] = jnp.concatenate([first[BLK:, HD:], second[BLK:, HD:]], axis=1)
        first, second = kv_ref[2 * t], kv_ref[2 * t + 1]
        dk_ref[:, columns] = jnp.concatenate([first[:, :HD], second[:, :HD]], axis=1)
        dv_ref[:, columns] = jnp.concatenate([first[:, HD:], second[:, HD:]], axis=1)
    marks = chosen(rank_ref[pl.ds(lax.axis_index("ctx"), 1), :])
    spread = contract(marks, compact[...], 0, 0).astype(jnp.bfloat16)
    crowded = jnp.broadcast_to(most_ref[:1, :1], spread.shape) > CAP - 0.5
    dq_ref[...] = jnp.where(crowded, full_ref[...], spread)


def spread(oq, kv, rank, most, full):
    vmem = pl.BlockSpec(memory_space=pltpu.VMEM)
    return pl.pallas_call(
        spread_kernel,
        out_shape=(jax.ShapeDtypeStruct(full.shape, full.dtype),) * 4,
        in_specs=[vmem] * 5,
        out_specs=(vmem,) * 4,
        scratch_shapes=[pltpu.VMEM((CAP, full.shape[1]), full.dtype)],
        compiler_params=pltpu.CompilerParams(vmem_limit_bytes=48 * 1024 * 1024),
        name="spread",
    )(oq, kv, rank, most, full)


def body(queries, keys, values, out_weight, cotangent, positions, global_blocks, random_blocks):
    rows_here = queries.shape[0]
    nz, nctx = lax.axis_size("fsdp"), lax.axis_size("ctx")
    local_blocks = nctx * rows_here // BLK
    kv, qg, rank, most = collect(
        nz, nctx, global_blocks, queries, keys, values, cotangent, out_weight, positions
    )
    crowded = most[0, 0] > CAP - 0.5

    def dense_gradient(qg):
        offset = (lax.axis_index("fsdp") * nctx + lax.axis_index("ctx")) * rows_here
        places = offset + jnp.arange(rows_here, dtype=jnp.int32)
        masked = jnp.any(positions[:, None] == places[None, :], axis=0)
        upstream = jnp.where(masked[:, None], cotangent, jnp.zeros_like(cotangent))
        weight = lax.all_gather(out_weight, "fsdp", axis=0, tiled=True)
        grad = contract(upstream, weight, 1, 1).astype(jnp.bfloat16)
        grad = lax.all_to_all(grad, "ctx", split_axis=1, concat_axis=0, tiled=True)
        return jnp.concatenate([qg[:, :HD], grad], axis=1)

    qg = lax.cond(crowded, dense_gradient, lambda qg: qg, qg)
    picks = random_blocks.transpose(2, 1, 0).reshape(random_blocks.shape[2], local_blocks)
    dqo, sums = attend(global_blocks, picks, kv, qg)
    parts, key_values = deliver(nz, nctx, rows_here, global_blocks, dqo, sums, rank)

    def dense_query():
        return lax.all_to_all(dqo[:, :HD], "ctx", split_axis=0, concat_axis=1, tiled=True)

    full = lax.cond(crowded, dense_query, lambda: jnp.zeros_like(queries))
    return spread(parts, key_values, rank, most, full)


def solution(mesh):
    split = P(("fsdp", "ctx"), None)
    return jax.shard_map(
        body,
        mesh=mesh,
        in_specs=(split, split, split, P("fsdp", None), split, P(), P(), P("fsdp", "ctx", None)),
        out_specs=(split, split, split, split),
        check_vma=False,
    )
```

time: 191 us -> 143 us (0.75)
  Pallas kernels: 163 us -> 121 us
  local copies, waits for them, and re-layouts: 11 us -> 5.36 us
    pallas_call x1, Pallas kernels: 55.9 us -> 32.4 us  [deliver(): pl.pallas_call(functools.partial(deliver_kernel, nz, nctx), out_shape=(ja...]
    pallas_call x1, Pallas kernels: 78.8 us -> 66.2 us  [collect(): pl.pallas_call(functools.partial(collect_kernel, nz, nctx), out_shape=(ja...]
    pallas_call x1 -> x2, Pallas kernels: 28.7 us -> 21.9 us  [the longest x1 19 us: attend(): pl.pallas_call(attend_kernel, out_shape=(jax.ShapeDtypeStruct(qg.shape, j...]
    unnamed x17 -> x19, local copies, waits for them, and re-layouts: 7.4 us -> 3.32 us
where the time goes in v3:
time: 143 us; the launch traced here: 141 us
  Pallas kernels  121 us (85%)
  between operations  14.8 us (10%)
  local copies, waits for them, and re-layouts  5.36 us (4%)
    pallas_call x1, Pallas kernels, collect(): pl.pallas_call(functools.partial(collect_kernel, nz, nctx), out_shape=(ja...  66.2 us
    pallas_call x1, Pallas kernels, deliver(): pl.pallas_call(functools.partial(deliver_kernel, nz, nctx), out_shape=(ja...  32.4 us
    pallas_call x1, Pallas kernels, attend(): pl.pallas_call(attend_kernel, out_shape=(jax.ShapeDtypeStruct(qg.shape, j...  19 us
    unnamed x19, local copies, waits for them, and re-layouts  3.32 us
    pallas_call x1, Pallas kernels, spread(): pl.pallas_call(spread_kernel, out_shape=(jax.ShapeDtypeStruct(full.shape,...  2.92 us

profile of v3, /device:TPU:1, one launch (start us, length us, event | category | flops | bytes accessed | tf_op | source)
XLA Modules:
  0.0 140.7 jit_solution(8511210281159366890)
XLA Ops:
  7.2 66.2 %collect.1 = (bf16[4352,128]{1,0:T(8,128)(2,1)}, bf16[4096,128]{1,0:T(8,128)(2,1)S(1)}, f32[32,128]{1,0:T(8,128)}, f32[8,128]{1,0:T(8,128)}) custom-call(s32[2]{0:T(128)} %glob_ref.5, bf16[128,2048]{1,0:T(8,128)(2,1)} %q_ref.1, bf16[128,2048]{1,0:T(8,128)(2,1)} %k_ref.1, bf16[128,2048]{1,0:T(8,128)(2,1)} %v_ref.1, bf16[128,2048]{1,0:T(8,128)(2,1)} %ct_ref.1, ...), custom_call_target="tpu_custom_call" | custom-call | tf_op jit(solution)/shard_map/collect/pallas_call | solution.py:583
  73.4 1.2 slice.9
  75.2 0.0 copy-start.8
  75.3 0.0 copy-start.1
  75.3 0.0 copy-start.5
  75.3 0.0 copy-start.7
  75.3 0.6 copy-done.8
  75.9 0.3 copy-done.7
  76.3 0.6 copy-done.1
  76.9 0.0 copy-done.5
  76.9 19.0 %attend.1 = (bf16[4096,128]{1,0:T(8,128)(2,1)S(1)}, bf16[4352,128]{1,0:T(8,128)(2,1)S(1)}) custom-call(s32[2]{0:T(128)S(1)} %copy-done.5, s32[3,64]{1,0:T(4,128)S(1)} %bitcast.23, bf16[4352,128]{1,0:T(8,128)(2,1)S(1)} %copy-done.1, bf16[4096,128]{1,0:T(8,128)(2,1)} %copy-done.7), custom_call_target="tpu_custom_call" | custom-call | tf_op jit(solution)/shard_map/attend/pallas_call | solution.py:127
  95.9 0.0 copy-start
  95.9 1.0 copy-done
  96.9 0.0 copy-start.4
  96.9 0.0 copy-start.6
  96.9 32.4 %deliver.1 = (bf16[32,80,128]{2,1,0:T(8,128)(2,1)}, bf16[32,128,128]{2,1,0:T(8,128)(2,1)}) custom-call(s32[2]{0:T(128)} %glob_ref.5, bf16[4096,128]{1,0:T(8,128)(2,1)S(1)} %get-tuple-element.35.dqo_ref, bf16[4352,128]{1,0:T(8,128)(2,1)} %copy-done, f32[32,128]{1,0:T(8,128)} %get-tuple-element.37.rank_ref), custom_call_target="tpu_custom_call" | custom-call | tf_op jit(solution)/shard_map/deliver/pallas_call | solution.py:752
  129.4 0.0 copy-start.2
  129.4 0.0 copy-start.3
  129.4 0.9 conditional.3
  129.4 0.9 broadcast.11.clone
  130.2 0.0 copy-done.4
  130.2 0.0 copy-done.6
  130.2 0.5 copy-done.2
  130.8 0.2 copy-done.3
  130.9 2.9 %spread.1 = (bf16[128,2048]{1,0:T(8,128)(2,1)}, bf16[128,2048]{1,0:T(8,128)(2,1)}, bf16[128,2048]{1,0:T(8,128)(2,1)}, bf16[128,2048]{1,0:T(8,128)(2,1)}) custom-call(bf16[32,80,128]{2,1,0:T(8,128)(2,1)S(1)} %copy-done.3, bf16[32,128,128]{2,1,0:T(8,128)(2,1)S(1)} %copy-done.2, f32[32,128]{1,0:T(8,128)S(1)} %copy-done.4, f32[8,128]{1,0:T(8,128)S(1)} %copy-done.6, ...), custom_call_target="tpu_custom_call" | custom-call | tf_op jit(solution)/shard_map/spread/pallas_call | solution.py:800
  (2 shorter events, 0.0 us)
Async XLA Ops:
  75.2 0.7 copy-start.8
  75.3 1.6 %copy-start.1 = (bf16[4352,128]{1,0:T(8,128)(2,1)S(1)}, bf16[4352,128]{1,0:T(8,128)(2,1)}, u32[]{:S(2)}) copy-start(bf16[4352,128]{1,0:T(8,128)(2,1)} %get-tuple-element.32.kv_ref) | copy-start | bytes 3342340
  75.3 1.6 %copy-start.5 = (s32[2]{0:T(128)S(1)}, s32[2]{0:T(128)}, u32[]{:S(2)}) copy-start(s32[2]{0:T(128)} %glob_ref.5) | copy-start | bytes 28
  75.3 1.0 copy-start.7
  95.9 1.0 copy-start
  96.9 33.3 %copy-start.4 = (f32[32,128]{1,0:T(8,128)S(1)}, f32[32,128]{1,0:T(8,128)}, u32[]{:S(2)}) copy-start(f32[32,128]{1,0:T(8,128)} %get-tuple-element.37.rank_ref) | copy-start | bytes 49156
  96.9 33.3 %copy-start.6 = (f32[8,128]{1,0:T(8,128)S(1)}, f32[8,128]{1,0:T(8,128)}, u32[]{:S(2)}) copy-start(f32[8,128]{1,0:T(8,128)} %get-tuple-element.33.most_ref) | copy-start | bytes 12292
  129.4 1.4 %copy-start.2 = (bf16[32,128,128]{2,1,0:T(8,128)(2,1)S(1)}, bf16[32,128,128]{2,1,0:T(8,128)(2,1)}, u32[]{:S(2)}) copy-start(bf16[32,128,128]{2,1,0:T(8,128)(2,1)} %get-tuple-element.39.kv_ref) | copy-start | bytes 3145732
  129.4 1.6 %copy-start.3 = (bf16[32,80,128]{2,1,0:T(8,128)(2,1)S(1)}, bf16[32,80,128]{2,1,0:T(8,128)(2,1)}, u32[]{:S(2)}) copy-start(bf16[32,80,128]{2,1,0:T(8,128)(2,1)} %get-tuple-element.38.oq_ref) | copy-start | bytes 1966084

commit v4 on v3

--- a/solution.py
+++ b/solution.py
@@ -251,16 +251,25 @@
 
 
 def collect_kernel(
-    nz, nctx, glob_ref, q_ref, k_ref, v_ref, ct_ref, w_ref, pos_ref,
+    nz, nctx, glob_ref, q_far, k_far, v_far, ct_far, w_ref, pos_ref,
     kv_ref, qg_ref, rank_ref, most_ref,
     kv_pack, q_pack, q_all, up_own, up_all, w_all, p_out, p_in, g_all, count, g_own, g_in, g_mid, g_out,
     kv_send, kv_recv, q_send, q_recv, up_send, up_recv, w_send, w_recv, a_send, a_recv, p_send, p_recv,
     edge_send, edge_recv, in_send, in_recv, out_send, out_recv, pair_send, pair_recv, own_sem,
+    q_ref, k_ref, v_ref, ct_ref, load_sem,
 ):
     z, c = place(nz, nctx)
     chip, core = c // 2, lax.rem(c, 2)
     cuts = square(nctx // 2)
     x, y = chip // cuts, lax.rem(chip, cuts)
+    loads = [
+        pltpu.make_async_copy(far, near, load_sem.at[i])
+        for i, (far, near) in enumerate(
+            [(k_far, k_ref), (v_far, v_ref), (q_far, q_ref), (ct_far, ct_ref)]
+        )
+    ]
+    for load in loads:
+        load.start()
     rows = q_ref.shape[0]
     wide = q_ref.shape[1]
     depth = wide // cuts
@@ -269,6 +278,8 @@
     partner = 2 * chip + 1 - core
     low = lax.broadcasted_iota(jnp.int32, (BLK, 2 * HD), 1) < HD
     greet(nz, nctx)
+    loads[0].wait()
+    loads[1].wait()
 
     for t in range(nctx // 2):
         columns = slice(2 * t * HD, 2 * (t + 1) * HD)
@@ -325,6 +336,8 @@
     lax.fori_loop(1, nctx, kv_go, 0)
     kv_ref[pl.ds(pl.multiple_of(BLK + c * rows, BLK), rows)] = kv_pack[c]
 
+    loads[2].wait()
+    loads[3].wait()
     for t in range(nctx // 2):
         columns = slice(2 * t * HD, 2 * (t + 1) * HD)
         top, bottom = q_ref[:BLK, columns], q_ref[BLK:, columns]
@@ -379,7 +392,7 @@
     rank = contract(masked.astype(jnp.bfloat16), jnp.where(before, 1.0, 0.0).astype(jnp.bfloat16), 1, 0)
     count[...] = jnp.where(masked > 0.5, rank, -1.0)
     most = jnp.max(jnp.max(count[...], axis=0, keepdims=True), axis=1, keepdims=True)
-    most_ref[...] = jnp.broadcast_to(most, most_ref.shape)
+    most_ref[0, 0] = jnp.max(most)
     rank_ref[...] = count[pl.ds(pl.multiple_of(z * nctx, nctx), nctx), :]
     mine = chosen(rank_ref[pl.ds(c, 1), :])
     up_own[...] = contract(mine, ct_ref[...], 1, 0).astype(jnp.bfloat16)
@@ -520,6 +533,17 @@
         total = total + g_out[e + 1].astype(jnp.float32)
     kv_ref[pl.ds((local_blocks + 2) * BLK, GLOB * BLK), :] = total.astype(jnp.bfloat16)
 
+    all_of(q_all.at[pl.ds(0, nctx - 1)], q_send, q_recv).wait_recv()
+    low_rows = lax.broadcasted_iota(jnp.int32, (rows, 2 * HD), 1) < HD
+
+    def lay(j, carry):
+        two = q_all[j]
+        begin = pl.multiple_of(j * rows, rows)
+        qg_ref[pl.ds(begin, BLK), :] = two
+        qg_ref[pl.ds(begin + BLK, BLK), :] = halves(two)
+        return carry
+
+    lax.fori_loop(0, nctx, lay, 0, unroll=4)
     grad = p_out[x]
     for e, copy in enumerate(partials):
         copy.wait_recv()
@@ -528,7 +552,6 @@
     swap_out = pair_copy(g_all.at[core], g_all.at[core], 1)
     swap_in = pair_copy(g_all.at[1 - core], g_all.at[1 - core], 1)
     swap_out.start()
-    all_of(q_all.at[pl.ds(0, nctx - 1)], q_send, q_recv).wait_recv()
     swap_in.wait_recv()
 
     def expand(j, carry):
@@ -536,10 +559,8 @@
         compact = g_all[lax.rem(j, 2), pl.ds(pl.multiple_of((j // 2) * CAP, CAP), CAP), :]
         dense = contract(marks, compact, 0, 0).astype(jnp.bfloat16)
         dense = jnp.where(jnp.full(dense.shape, core == 0), halves(dense), dense)
-        two = q_all[j]
-        begin = pl.multiple_of(j * rows, rows)
-        qg_ref[pl.ds(begin, BLK), :] = jnp.where(low, two, dense[:BLK])
-        qg_ref[pl.ds(begin + BLK, BLK), :] = jnp.where(low, halves(two), dense[BLK:])
+        at = pl.ds(pl.multiple_of(j * rows, rows), rows)
+        qg_ref[at, :] = jnp.where(low_rows, qg_ref[at, :], dense)
         return carry
 
     lax.fori_loop(0, nctx, expand, 0, unroll=4)
@@ -586,10 +607,12 @@
             jax.ShapeDtypeStruct((region + (2 + GLOB) * BLK, 2 * HD), half),
             jax.ShapeDtypeStruct((region, 2 * HD), half),
             jax.ShapeDtypeStruct((nctx, rows), jnp.float32),
-            jax.ShapeDtypeStruct((8, 128), jnp.float32),
+            jax.ShapeDtypeStruct((1, 1), jnp.float32),
         ),
-        in_specs=[pl.BlockSpec(memory_space=pltpu.SMEM)] + [vmem] * 6,
-        out_specs=(vmem,) * 4,
+        in_specs=[pl.BlockSpec(memory_space=pltpu.SMEM)]
+        + [pl.BlockSpec(memory_space=pl.ANY)] * 5
+        + [vmem],
+        out_specs=(vmem, vmem, vmem, pl.BlockSpec(memory_space=pltpu.SMEM)),
         scratch_shapes=[
             pltpu.VMEM((nctx, rows, 2 * HD), half),
             pltpu.VMEM((nctx, BLK, 2 * HD), half),
@@ -610,6 +633,8 @@
             dma((2,)), dma((2,)),
             dma((side,)), dma((side,)), dma((nz // side,)), dma((nz // side,)),
             dma((2,)), dma((2,)), dma(()),
+            pltpu.VMEM((rows, wide), half), pltpu.VMEM((rows, wide), half),
+            pltpu.VMEM((rows, wide), half), pltpu.VMEM((rows, wide), half), dma((4,)),
         ],
         compiler_params=pltpu.CompilerParams(
             collective_id=0, has_side_effects=True, vmem_limit_bytes=56 * 1024 * 1024
@@ -619,10 +644,11 @@
 
 
 def deliver_kernel(
-    nz, nctx, glob_ref, dqo_ref, sums_ref, rank_ref,
+    nz, nctx, glob_ref, dqo_far, sums_far, rank_ref,
     oq_all, kv_all,
     oq_pack, kv_pack, edge_out, edge_in, g_own, g_in, g_mid, g_out,
     oq_send, oq_recv, kv_send, kv_recv, edge_send, edge_recv, in_send, in_recv, out_send, out_recv,
+    dqo_ref, sums_ref, load_sem,
 ):
     z, c = place(nz, nctx)
     rows = kv_all.shape[1]
@@ -630,10 +656,17 @@
     local_blocks = nctx * rows // BLK
     few = CAP // 2
     high_begin = (local_blocks + 1) * BLK
+    load_sums = pltpu.make_async_copy(sums_far, sums_ref, load_sem.at[0])
+    load_rows = pltpu.make_async_copy(dqo_far, dqo_ref, load_sem.at[1])
+    load_sums.start()
+    load_rows.start()
     greet(nz, nctx)
+    load_sums.wait()
     edge_out[0] = sums_ref[pl.ds(0, BLK), :]
     edge_out[1] = sums_ref[pl.ds(high_begin, BLK), :]
     g_own[...] = sums_ref[pl.ds(high_begin + BLK, GLOB * BLK), :]
+
+    load_rows.wait()
 
     def shrink(j, carry):
         both = dqo_ref[pl.ds(pl.multiple_of(j * rows, rows), rows), :]
@@ -703,7 +736,7 @@
         total = total + g_out[e].astype(jnp.float32)
     wanted = [glob_ref[i] - z * local_blocks for i in range(GLOB)]
 
-    def settle(j, carry):
+    def settle(j):
         for side_of in range(2):
             b = 2 * j + side_of
             term = sums_ref[pl.ds(pl.multiple_of((b + 1) * BLK, BLK), BLK), :].astype(jnp.float32)
@@ -714,17 +747,16 @@
             at_edge = j == (nctx - 1) * side_of
             term = term + jnp.where(jnp.full(edge.shape, at_edge), edge, 0.0)
             kv_pack[j, pl.ds(side_of * BLK, BLK), :] = term.astype(jnp.bfloat16)
-        return carry
-
-    lax.fori_loop(0, nctx, settle, 0, unroll=2)
 
     def kv_go(d, carry):
+        settle(lax.rem(c + d, nctx))
         plane_copy(
             nz, nctx, d, lambda p: kv_pack.at[p], lambda s: kv_all.at[s], kv_send, kv_recv
         ).start()
         return carry
 
     lax.fori_loop(1, nctx, kv_go, 0)
+    settle(c)
     kv_all[c] = kv_pack[c]
 
     all_of(oq_all.at[pl.ds(0, nctx - 1)], oq_send, oq_recv).wait_recv()
@@ -755,7 +787,9 @@
             jax.ShapeDtypeStruct((nctx, BLK + CAP // 2, 2 * HD), half),
             jax.ShapeDtypeStruct((nctx, rows, 2 * HD), half),
         ),
-        in_specs=[pl.BlockSpec(memory_space=pltpu.SMEM)] + [vmem] * 3,
+        in_specs=[pl.BlockSpec(memory_space=pltpu.SMEM)]
+        + [pl.BlockSpec(memory_space=pl.ANY)] * 2
+        + [vmem],
         out_specs=(vmem,) * 2,
         scratch_shapes=[
             pltpu.VMEM((nctx, BLK + CAP // 2, 2 * HD), half),
@@ -769,6 +803,7 @@
             dma(()), dma(()), dma(()), dma(()),
             dma((2,)), dma((2,)),
             dma((side,)), dma((side,)), dma((nz // side,)), dma((nz // side,)),
+            pltpu.VMEM(dqo.shape, half), pltpu.VMEM(sums.shape, half), dma((2,)),
         ],
         compiler_params=pltpu.CompilerParams(
             collective_id=1, has_side_effects=True, vmem_limit_bytes=56 * 1024 * 1024
@@ -791,7 +826,7 @@
         dv_ref[:, columns] = jnp.concatenate([first[:, HD:], second[:, HD:]], axis=1)
     marks = chosen(rank_ref[pl.ds(lax.axis_index("ctx"), 1), :])
     spread = contract(marks, compact[...], 0, 0).astype(jnp.bfloat16)
-    crowded = jnp.broadcast_to(most_ref[:1, :1], spread.shape) > CAP - 0.5
+    crowded = jnp.full(spread.shape, most_ref[0, 0]) > CAP - 0.5
     dq_ref[...] = jnp.where(crowded, full_ref[...], spread)
 
 
@@ -800,7 +835,7 @@
     return pl.pallas_call(
         spread_kernel,
         out_shape=(jax.ShapeDtypeStruct(full.shape, full.dtype),) * 4,
-        in_specs=[vmem] * 5,
+        in_specs=[vmem, vmem, vmem, pl.BlockSpec(memory_space=pltpu.SMEM), vmem],
         out_specs=(vmem,) * 4,
         scratch_shapes=[pltpu.VMEM((CAP, full.shape[1]), full.dtype)],
         compiler_params=pltpu.CompilerParams(vmem_limit_bytes=48 * 1024 * 1024),

time: 143 us -> 141 us (0.986)
    unnamed x19 -> x17, local copies, waits for them, and re-layouts: 3.32 us -> 3.31 us
where the time goes in v4:
time: 141 us; the launch traced here: 138 us
  Pallas kernels  120 us (85%)
  between operations  14.7 us (10%)
  local copies, waits for them, and re-layouts  4.17 us (3%)
    pallas_call x1, Pallas kernels, collect(): pl.pallas_call(functools.partial(collect_kernel, nz, nctx), out_shape=(ja...  65 us
    pallas_call x1, Pallas kernels, deliver(): pl.pallas_call(functools.partial(deliver_kernel, nz, nctx), out_shape=(ja...  32.2 us
    pallas_call x1, Pallas kernels, attend(): pl.pallas_call(attend_kernel, out_shape=(jax.ShapeDtypeStruct(qg.shape, j...  19 us
    pallas_call x1, Pallas kernels, spread(): pl.pallas_call(spread_kernel, out_shape=(jax.ShapeDtypeStruct(full.shape,...  3.48 us
    unnamed x17, local copies, waits for them, and re-layouts  3.31 us

profile of v4, /device:TPU:1, one launch (start us, length us, event | category | flops | bytes accessed | tf_op | source)
XLA Modules:
  0.0 138.5 jit_solution(8133515594609700751)
XLA Ops:
  7.2 65.0 %collect.1 = (bf16[4352,128]{1,0:T(8,128)(2,1)}, bf16[4096,128]{1,0:T(8,128)(2,1)S(1)}, f32[32,128]{1,0:T(8,128)}, f32[1,1]{1,0:T(1,128)}) custom-call(s32[2]{0:T(128)} %glob_ref.5, bf16[128,2048]{1,0:T(8,128)(2,1)} %q_far.1, bf16[128,2048]{1,0:T(8,128)(2,1)} %k_far.1, bf16[128,2048]{1,0:T(8,128)(2,1)} %v_far.1, bf16[128,2048]{1,0:T(8,128)(2,1)} %ct_far.1, ...), custom_call_target="tpu_custom_call" | custom-call | tf_op jit(solution)/shard_map/collect/pallas_call | solution.py:604
  72.7 0.0 copy-start.7
  72.7 0.0 copy-start.1
  72.8 0.0 copy-start.5
  72.8 0.0 copy-start.6
  72.8 0.6 copy-done.7
  73.4 0.3 copy-done.6
  73.8 0.6 copy-done.1
  74.4 0.0 copy-done.5
  74.4 19.0 %attend.1 = (bf16[4096,128]{1,0:T(8,128)(2,1)S(1)}, bf16[4352,128]{1,0:T(8,128)(2,1)S(1)}) custom-call(s32[2]{0:T(128)S(1)} %copy-done.5, s32[3,64]{1,0:T(4,128)S(1)} %bitcast.23, bf16[4352,128]{1,0:T(8,128)(2,1)S(1)} %copy-done.1, bf16[4096,128]{1,0:T(8,128)(2,1)} %copy-done.6), custom_call_target="tpu_custom_call" | custom-call | tf_op jit(solution)/shard_map/attend/pallas_call | solution.py:127
  93.4 0.0 copy-start
  93.4 1.0 copy-done
  94.4 0.0 copy-start.4
  94.4 32.2 %deliver.1 = (bf16[32,80,128]{2,1,0:T(8,128)(2,1)}, bf16[32,128,128]{2,1,0:T(8,128)(2,1)}) custom-call(s32[2]{0:T(128)} %glob_ref.5, bf16[4096,128]{1,0:T(8,128)(2,1)S(1)} %get-tuple-element.35.dqo_far, bf16[4352,128]{1,0:T(8,128)(2,1)} %copy-done, f32[32,128]{1,0:T(8,128)} %get-tuple-element.37.rank_ref), custom_call_target="tpu_custom_call" | custom-call | tf_op jit(solution)/shard_map/deliver/pallas_call | solution.py:784
  126.6 0.0 copy-start.2
  126.6 0.0 copy-start.3
  126.6 0.9 conditional.3
  126.6 0.9 broadcast.11.clone
  127.5 0.0 copy-done.4
  127.5 0.5 copy-done.2
  128.0 0.2 copy-done.3
  128.2 3.5 %spread.1 = (bf16[128,2048]{1,0:T(8,128)(2,1)}, bf16[128,2048]{1,0:T(8,128)(2,1)}, bf16[128,2048]{1,0:T(8,128)(2,1)}, bf16[128,2048]{1,0:T(8,128)(2,1)}) custom-call(bf16[32,80,128]{2,1,0:T(8,128)(2,1)S(1)} %copy-done.3, bf16[32,128,128]{2,1,0:T(8,128)(2,1)S(1)} %copy-done.2, f32[32,128]{1,0:T(8,128)S(1)} %copy-done.4, f32[1,1]{1,0:T(1,128)} %get-tuple-element.33.most_ref, ...), custom_call_target="tpu_custom_call" | custom-call | tf_op jit(solution)/shard_map/spread/pallas_call | solution.py:835
  (2 shorter events, 0.0 us)
Async XLA Ops:
  72.7 0.7 copy-start.7
  72.7 1.6 %copy-start.1 = (bf16[4352,128]{1,0:T(8,128)(2,1)S(1)}, bf16[4352,128]{1,0:T(8,128)(2,1)}, u32[]{:S(2)}) copy-start(bf16[4352,128]{1,0:T(8,128)(2,1)} %get-tuple-element.32.kv_ref) | copy-start | bytes 3342340
  72.8 1.6 %copy-start.5 = (s32[2]{0:T(128)S(1)}, s32[2]{0:T(128)}, u32[]{:S(2)}) copy-start(s32[2]{0:T(128)} %glob_ref.5) | copy-start | bytes 28
  72.8 1.0 copy-start.6
  93.4 1.0 copy-start
  94.4 33.1 %copy-start.4 = (f32[32,128]{1,0:T(8,128)S(1)}, f32[32,128]{1,0:T(8,128)}, u32[]{:S(2)}) copy-start(f32[32,128]{1,0:T(8,128)} %get-tuple-element.37.rank_ref) | copy-start | bytes 49156
  126.6 1.4 %copy-start.2 = (bf16[32,128,128]{2,1,0:T(8,128)(2,1)S(1)}, bf16[32,128,128]{2,1,0:T(8,128)(2,1)}, u32[]{:S(2)}) copy-start(bf16[32,128,128]{2,1,0:T(8,128)(2,1)} %get-tuple-element.39.kv_ref) | copy-start | bytes 3145732
  126.6 1.6 %copy-start.3 = (bf16[32,80,128]{2,1,0:T(8,128)(2,1)S(1)}, bf16[32,80,128]{2,1,0:T(8,128)(2,1)}, u32[]{:S(2)}) copy-start(bf16[32,80,128]{2,1,0:T(8,128)(2,1)} %get-tuple-element.38.oq_ref) | copy-start | bytes 1966084

commit v5 on v4

--- a/solution.py
+++ b/solution.py
@@ -369,31 +369,31 @@
 
     lax.fori_loop(1, nz, weight_go, 0)
 
-    devices = nz * nctx
-    count[...] = jnp.zeros_like(count)
     span = 2 * pos_ref.shape[1]
-    group_ids = lax.broadcasted_iota(jnp.int32, (devices, span), 0)
     inside_ids = lax.broadcasted_iota(jnp.int32, (rows, span), 0)
-
-    def tally(i, carry):
+    before = lax.broadcasted_iota(jnp.int32, (rows, rows), 0) < lax.broadcasted_iota(
+        jnp.int32, (rows, rows), 1
+    )
+    before = jnp.where(before, 1.0, 0.0).astype(jnp.bfloat16)
+
+    def tally(i, first, groups):
         pos = jnp.concatenate([pos_ref[pl.ds(2 * i, 1), :], pos_ref[pl.ds(2 * i + 1, 1), :]], axis=1)
         group = pos // rows
-        inside = pos - group * rows
-        hit = jnp.where(group_ids == group, 1.0, 0.0).astype(jnp.bfloat16)
-        spot = jnp.where(inside_ids == inside, 1.0, 0.0).astype(jnp.bfloat16)
-        count[...] += contract(hit, spot, 1, 1)
-        return carry
-
-    lax.fori_loop(0, pos_ref.shape[0] // 2, tally, 0)
-    masked = jnp.where(count[...] > 0.5, 1.0, 0.0)
-    before = lax.broadcasted_iota(jnp.int32, (rows, rows), 0) < lax.broadcasted_iota(
-        jnp.int32, (rows, rows), 1
-    )
-    rank = contract(masked.astype(jnp.bfloat16), jnp.where(before, 1.0, 0.0).astype(jnp.bfloat16), 1, 0)
-    count[...] = jnp.where(masked > 0.5, rank, -1.0)
-    most = jnp.max(jnp.max(count[...], axis=0, keepdims=True), axis=1, keepdims=True)
-    most_ref[0, 0] = jnp.max(most)
-    rank_ref[...] = count[pl.ds(pl.multiple_of(z * nctx, nctx), nctx), :]
+        ids = lax.broadcasted_iota(jnp.int32, (groups, span), 0) + first
+        hit = jnp.where(ids == group, 1.0, 0.0).astype(jnp.bfloat16)
+        spot = jnp.where(inside_ids == pos - group * rows, 1.0, 0.0).astype(jnp.bfloat16)
+        return contract(hit, spot, 1, 1)
+
+    def ranks(counts):
+        masked = jnp.where(counts > 0.5, 1.0, 0.0)
+        return jnp.where(masked > 0.5, contract(masked.astype(jnp.bfloat16), before, 1, 0), -1.0)
+
+    rank_ref[...] = ranks(
+        lax.fori_loop(
+            0, pos_ref.shape[0] // 2, lambda i, total: total + tally(i, z * nctx, nctx),
+            jnp.zeros((nctx, rows), jnp.float32), unroll=4,
+        )
+    )
     mine = chosen(rank_ref[pl.ds(c, 1), :])
     up_own[...] = contract(mine, ct_ref[...], 1, 0).astype(jnp.bfloat16)
 
@@ -508,6 +508,15 @@
     partials = [partial_copy(e) for e in range(1, cuts)]
     for copy in partials:
         copy.start()
+
+    count[...] = jnp.zeros_like(count)
+
+    def tally_all(i, carry):
+        count[...] += tally(i, 0, nz * nctx)
+        return carry
+
+    lax.fori_loop(0, pos_ref.shape[0] // 2, tally_all, 0)
+    most_ref[0, 0] = jnp.max(ranks(count[...]))
 
     @pl.when(z > 0)
     def _():

time: 141 us -> 141 us (level)
  no operation moved by 1% of the time
where the time goes in v5:
time: 141 us; the launch traced here: 139 us
  Pallas kernels  120 us (85%)
  between operations  14.7 us (10%)
  local copies, waits for them, and re-layouts  4.17 us (3%)
    pallas_call x1, Pallas kernels, collect(): pl.pallas_call(functools.partial(collect_kernel, nz, nctx), out_shape=(ja...  65.3 us
    pallas_call x1, Pallas kernels, deliver(): pl.pallas_call(functools.partial(deliver_kernel, nz, nctx), out_shape=(ja...  32.3 us
    pallas_call x1, Pallas kernels, attend(): pl.pallas_call(attend_kernel, out_shape=(jax.ShapeDtypeStruct(qg.shape, j...  19 us
    pallas_call x1, Pallas kernels, spread(): pl.pallas_call(spread_kernel, out_shape=(jax.ShapeDtypeStruct(full.shape,...  3.48 us
    unnamed x17, local copies, waits for them, and re-layouts  3.31 us

profile of v5, /device:TPU:1, one launch (start us, length us, event | category | flops | bytes accessed | tf_op | source)
XLA Modules:
  0.0 138.9 jit_solution(14026685090401907934)
XLA Ops:
  7.2 65.3 %collect.1 = (bf16[4352,128]{1,0:T(8,128)(2,1)}, bf16[4096,128]{1,0:T(8,128)(2,1)S(1)}, f32[32,128]{1,0:T(8,128)}, f32[1,1]{1,0:T(1,128)}) custom-call(s32[2]{0:T(128)} %glob_ref.5, bf16[128,2048]{1,0:T(8,128)(2,1)} %q_far.1, bf16[128,2048]{1,0:T(8,128)(2,1)} %k_far.1, bf16[128,2048]{1,0:T(8,128)(2,1)} %v_far.1, bf16[128,2048]{1,0:T(8,128)(2,1)} %ct_far.1, ...), custom_call_target="tpu_custom_call" | custom-call | tf_op jit(solution)/shard_map/collect/pallas_call | solution.py:613
  73.0 0.0 copy-start.7
  73.0 0.0 copy-start.1
  73.0 0.0 copy-start.5
  73.1 0.0 copy-start.6
  73.1 0.6 copy-done.7
  73.7 0.3 copy-done.6
  74.0 0.6 copy-done.1
  74.7 0.0 copy-done.5
  74.7 19.0 %attend.1 = (bf16[4096,128]{1,0:T(8,128)(2,1)S(1)}, bf16[4352,128]{1,0:T(8,128)(2,1)S(1)}) custom-call(s32[2]{0:T(128)S(1)} %copy-done.5, s32[3,64]{1,0:T(4,128)S(1)} %bitcast.23, bf16[4352,128]{1,0:T(8,128)(2,1)S(1)} %copy-done.1, bf16[4096,128]{1,0:T(8,128)(2,1)} %copy-done.6), custom_call_target="tpu_custom_call" | custom-call | tf_op jit(solution)/shard_map/attend/pallas_call | solution.py:127
  93.7 0.0 copy-start
  93.7 1.0 copy-done
  94.7 0.0 copy-start.4
  94.7 32.3 %deliver.1 = (bf16[32,80,128]{2,1,0:T(8,128)(2,1)}, bf16[32,128,128]{2,1,0:T(8,128)(2,1)}) custom-call(s32[2]{0:T(128)} %glob_ref.5, bf16[4096,128]{1,0:T(8,128)(2,1)S(1)} %get-tuple-element.35.dqo_far, bf16[4352,128]{1,0:T(8,128)(2,1)} %copy-done, f32[32,128]{1,0:T(8,128)} %get-tuple-element.37.rank_ref), custom_call_target="tpu_custom_call" | custom-call | tf_op jit(solution)/shard_map/deliver/pallas_call | solution.py:793
  127.0 0.0 copy-start.2
  127.0 0.0 copy-start.3
  127.0 0.9 conditional.3
  127.0 0.9 broadcast.11.clone
  127.9 0.0 copy-done.4
  127.9 0.5 copy-done.2
  128.4 0.2 copy-done.3
  128.6 3.5 %spread.1 = (bf16[128,2048]{1,0:T(8,128)(2,1)}, bf16[128,2048]{1,0:T(8,128)(2,1)}, bf16[128,2048]{1,0:T(8,128)(2,1)}, bf16[128,2048]{1,0:T(8,128)(2,1)}) custom-call(bf16[32,80,128]{2,1,0:T(8,128)(2,1)S(1)} %copy-done.3, bf16[32,128,128]{2,1,0:T(8,128)(2,1)S(1)} %copy-done.2, f32[32,128]{1,0:T(8,128)S(1)} %copy-done.4, f32[1,1]{1,0:T(1,128)} %get-tuple-element.33.most_ref, ...), custom_call_target="tpu_custom_call" | custom-call | tf_op jit(solution)/shard_map/spread/pallas_call | solution.py:844
  (2 shorter events, 0.0 us)
Async XLA Ops:
  73.0 0.7 copy-start.7
  73.0 1.6 %copy-start.1 = (bf16[4352,128]{1,0:T(8,128)(2,1)S(1)}, bf16[4352,128]{1,0:T(8,128)(2,1)}, u32[]{:S(2)}) copy-start(bf16[4352,128]{1,0:T(8,128)(2,1)} %get-tuple-element.32.kv_ref) | copy-start | bytes 3342340
  73.0 1.6 %copy-start.5 = (s32[2]{0:T(128)S(1)}, s32[2]{0:T(128)}, u32[]{:S(2)}) copy-start(s32[2]{0:T(128)} %glob_ref.5) | copy-start | bytes 28
  73.1 1.0 copy-start.6
  93.7 1.0 copy-start
  94.7 33.2 %copy-start.4 = (f32[32,128]{1,0:T(8,128)S(1)}, f32[32,128]{1,0:T(8,128)}, u32[]{:S(2)}) copy-start(f32[32,128]{1,0:T(8,128)} %get-tuple-element.37.rank_ref) | copy-start | bytes 49156
  127.0 1.4 %copy-start.2 = (bf16[32,128,128]{2,1,0:T(8,128)(2,1)S(1)}, bf16[32,128,128]{2,1,0:T(8,128)(2,1)}, u32[]{:S(2)}) copy-start(bf16[32,128,128]{2,1,0:T(8,128)(2,1)} %get-tuple-element.39.kv_ref) | copy-start | bytes 3145732
  127.0 1.6 %copy-start.3 = (bf16[32,80,128]{2,1,0:T(8,128)(2,1)S(1)}, bf16[32,80,128]{2,1,0:T(8,128)(2,1)}, u32[]{:S(2)}) copy-start(bf16[32,80,128]{2,1,0:T(8,128)(2,1)} %get-tuple-element.38.oq_ref) | copy-start | bytes 1966084
